TPU v7x, 256 devices: a whole 4x4x8 slice. The times are simulated.
256 devices in a mesh: dp: 4 (over x), neuron: 8 (over z), expert: 8 (over y, core).
Axes of the slice: x: 4, y: 4, z: 8, core: 2. Of those that a mesh axis runs over, the one named last changes fastest.
Arguments:
- tokens: bfloat16 [512, 8192], P(('neuron', 'expert'), 'dp'), may hold values from -6 to 6
- teacher_gate: bfloat16 [28672, 8192], P(('neuron', 'expert'), 'dp'), may hold values from -0.0625 to 0.0625
- teacher_up: bfloat16 [28672, 8192], P(('neuron', 'expert'), 'dp'), may hold values from -0.0625 to 0.0625
- teacher_down: bfloat16 [28672, 8192], P(('neuron', 'expert'), 'dp'), may hold values from -0.03125 to 0.03125
- student_gate: bfloat16 [8, 1792, 8192], P('expert', 'neuron', 'dp'), may hold values from -0.0625 to 0.0625
- student_up: bfloat16 [8, 1792, 8192], P('expert', 'neuron', 'dp'), may hold values from -0.0625 to 0.0625
- student_down: bfloat16 [8, 1792, 8192], P('expert', 'neuron', 'dp'), may hold values from -0.125 to 0.125
- routes: int32 [512, 2], replicated, may hold values from 0 to 7, all different within a row; in each aligned block of 8 rows (0 to 7, 8 to 15, ...) at most 6 rows name the same one
- route_weight: float32 [512, 2], replicated, may hold values from 0.25 to 1
Outputs:
- grad_gate: bfloat16 [8, 1792, 8192], P('expert', 'neuron', 'dp')
- grad_up: bfloat16 [8, 1792, 8192], P('expert', 'neuron', 'dp')
- grad_down: bfloat16 [8, 1792, 8192], P('expert', 'neuron', 'dp')
Inputs may be any that keep to these rules, and one draw needn't show every extreme that they name: `routes`: each token names 2 different experts. In each aligned block of 8 tokens (the tokens of one index of neuron and expert) no expert is named by more than 6 tokens, a bound that some block reaches.
All inputs are finite; a program needn't handle non-finite values.
Results may differ from a plain program's by a relative error of at most 0.008.
Values may be sent and summed in bfloat16 or wider, within the bound.
A program may use at most 128 MiB of HBM per device.

v0:
```python
import jax
import jax.numpy as jnp
from jax import lax
from jax.sharding import PartitionSpec as P

TOP = 2
MOST = 6


def block_selector(route_rows, weight_rows, expert_ids, slot_count):
    chosen = route_rows[None] == expert_ids[:, None, None, None]
    picked = jnp.any(chosen, axis=3).astype(jnp.int32)
    mixing = jnp.sum(jnp.where(chosen, weight_rows[None], jnp.zeros((), jnp.float32)), axis=3)
    ranked = jnp.cumsum(picked, axis=2) - picked
    slot_ids = jnp.arange(slot_count, dtype=jnp.int32)
    selector = (picked[:, :, None, :] == 1) & (
        ranked[:, :, None, :] == slot_ids[None, None, :, None]
    )
    return (selector.astype(jnp.float32), mixing)


def teacher_term(teacher_hidden, teacher_down):
    return lax.dot_general(
        teacher_hidden, teacher_down, (((0,), (0,)), ((), ())), preferred_element_type=jnp.float32
    )


def target_rows(teacher_hidden, teacher_down):
    return lax.psum_scatter(
        teacher_term(teacher_hidden, teacher_down),
        ("neuron", "expert"),
        scatter_dimension=0,
        tiled=True,
    )


def student_term(selector, weighted_blocks, width, length):
    combined = jnp.einsum(
        "kbmr,kbmd->brd", selector, weighted_blocks, precision=lax.Precision.HIGHEST
    )
    return combined.reshape(length, width)


def spread_residual(residual, selector_half, owners, row_count, width, local_experts, slot_count):
    every_residual = lax.all_gather(residual, ("neuron", "expert"), axis=0, tiled=True)
    residual_blocks = every_residual.reshape(owners, row_count, width)
    return (
        jnp.einsum(
            "kbmr,brd->kbmd", selector_half, residual_blocks, preferred_element_type=jnp.float32
        )
        .astype(jnp.bfloat16)
        .reshape(local_experts, owners * slot_count, width)
    )


def body(
    tokens,
    teacher_gate,
    teacher_up,
    teacher_down,
    student_gate,
    student_up,
    student_down,
    routes,
    route_weight,
):
    row_count = tokens.shape[0]
    width = tokens.shape[1]
    neurons = lax.axis_size("neuron")
    expert_groups = lax.axis_size("expert")
    owners = neurons * expert_groups
    local_experts = student_gate.shape[0]
    slot_count = MOST
    contract = (((1,), (1,)), ((), ()))
    gathered = lax.all_gather(tokens, ("neuron", "expert"), axis=0, tiled=True)
    teacher_pre = lax.dot_general(
        teacher_gate, gathered, contract, preferred_element_type=jnp.float32
    )
    teacher_lift = lax.dot_general(
        teacher_up, gathered, contract, preferred_element_type=jnp.float32
    )
    pre_whole, lift_whole = lax.psum((teacher_pre, teacher_lift), "dp")
    teacher_hidden = (jax.nn.silu(pre_whole) * lift_whole).astype(jnp.bfloat16)
    route_rows = routes.reshape(owners, row_count, TOP)
    weight_rows = route_weight.reshape(owners, row_count, TOP)
    expert_ids = lax.axis_index("expert") * local_experts + jnp.arange(
        local_experts, dtype=jnp.int32
    )
    selector, mixing = block_selector(route_rows, weight_rows, expert_ids, slot_count)
    selector_half = selector.astype(jnp.bfloat16)
    slot_mixing = jnp.einsum(
        "kbmr,kbr->kbm", selector, mixing, precision=lax.Precision.HIGHEST
    ).reshape(local_experts, owners * slot_count)
    token_blocks = gathered.reshape(owners, row_count, width)
    slot_tokens = (
        jnp.einsum(
            "kbmr,brd->kbmd", selector_half, token_blocks, preferred_element_type=jnp.float32
        )
        .astype(jnp.bfloat16)
        .reshape(local_experts, owners * slot_count, width)
    )
    batched = (((2,), (2,)), ((0,), (0,)))
    pre_part = lax.dot_general(
        student_gate, slot_tokens, batched, preferred_element_type=jnp.float32
    )
    lift_part = lax.dot_general(
        student_up, slot_tokens, batched, preferred_element_type=jnp.float32
    )
    expert_pre, expert_lift = lax.psum((pre_part, lift_part), "dp")
    sigmoid_part = jax.nn.sigmoid(expert_pre)
    activated = expert_pre * sigmoid_part
    expert_hidden = (activated * expert_lift).astype(jnp.bfloat16)
    output_part = lax.dot_general(
        expert_hidden,
        student_down,
        (((1,), (1,)), ((0,), (0,))),
        preferred_element_type=jnp.float32,
    )
    weighted = output_part * slot_mixing[:, :, None]
    weighted_blocks = weighted.reshape(local_experts, owners, slot_count, width)
    target = target_rows(teacher_hidden, teacher_down)
    student = lax.psum_scatter(
        student_term(
            selector, weighted_blocks, width, row_count * lax.axis_size(("neuron", "expert"))
        ),
        ("neuron", "expert"),
        scatter_dimension=0,
        tiled=True,
    )
    residual = (student - target).astype(jnp.bfloat16)
    slot_residual = spread_residual(
        residual, selector_half, owners, row_count, width, local_experts, slot_count
    )
    slot_grad = (slot_residual.astype(jnp.float32) * slot_mixing[:, :, None]).astype(jnp.bfloat16)
    slots_batched = (((2,), (1,)), ((0,), (0,)))
    grad_down = lax.dot_general(
        expert_hidden, slot_grad, slots_batched, preferred_element_type=jnp.float32
    ).astype(jnp.bfloat16)
    hidden_part = lax.dot_general(
        student_down, slot_grad, batched, preferred_element_type=jnp.float32
    )
    hidden_total = lax.psum(hidden_part, "dp")
    slope = sigmoid_part * (1.0 + expert_pre * (1.0 - sigmoid_part))
    pre_grad = (hidden_total * expert_lift * slope).astype(jnp.bfloat16)
    lift_grad = (hidden_total * activated).astype(jnp.bfloat16)
    grad_gate = lax.dot_general(
        pre_grad, slot_tokens, slots_batched, preferred_element_type=jnp.float32
    ).astype(jnp.bfloat16)
    grad_up = lax.dot_general(
        lift_grad, slot_tokens, slots_batched, preferred_element_type=jnp.float32
    ).astype(jnp.bfloat16)
    return (grad_gate, grad_up, grad_down)


def solution(mesh):
    return jax.shard_map(
        body,
        mesh=mesh,
        in_specs=(
            P(("neuron", "expert"), "dp"),
            P(("neuron", "expert"), "dp"),
            P(("neuron", "expert"), "dp"),
            P(("neuron", "expert"), "dp"),
            P("expert", "neuron", "dp"),
            P("expert", "neuron", "dp"),
            P("expert", "neuron", "dp"),
            P(),
            P(),
        ),
        out_specs=(
            P("expert", "neuron", "dp"),
            P("expert", "neuron", "dp"),
            P("expert", "neuron", "dp"),
        ),
        check_vma=False,
    )
```

profile of v0, /device:TPU:1, one launch (start us, length us, event | category | flops | bytes accessed | tf_op | source)
XLA Modules:
  0.0 551.6 jit_solution(6705202522019443692)
XLA Ops:
  7.2 0.0 copy-start
  7.2 0.0 all-gather.3.cloned.1.call-start
  7.2 0.7 all-gather.3.cloned.1.call-update
  7.9 0.0 all-reduce.12.cloned.1.call-start
  8.0 0.7 fusion.43
  8.7 0.1 reshape.225
  8.8 0.2 reduce_window_sum.11
  9.0 83.4 %all-gather.3.cloned.1.call-done = bf16[512,2048]{1,0:T(8,128)(2,1)} async-done(((bf16[8,2048]{1,0:T(8,128)(2,1)}), bf16[512,2048]{1,0:T(8,128)(2,1)}) %all-gather.3.cloned.1.call-update) | async-done | bytes 2097168 | tf_op jit(solution)/shard_map/all_gather | solution.py:75
  92.3 3.6 fusion
  96.0 2.6 reshape.214
  98.6 2.8 convolution_bitcast_fusion.1
  101.4 1.4 convolution_bitcast_fusion.2
  102.8 0.2 copy-done.2
  103.0 2.1 fusion.44
  105.0 2.1 fusion.45
  107.1 0.0 all-reduce.12.cloned.1.call-update
  107.1 0.0 all-reduce.10.cloned.1.call-start
  107.2 0.6 copy-done.8
  107.8 0.0 copy-done.9
  107.8 0.1 reshape.228
  107.9 0.4 fusion.24
  108.3 0.1 mul.70
  108.4 67.3 %all-reduce.12.cloned.1.call-done = (f32[1,224,384]{2,1,0:T(8,128)}, f32[448,512]{1,0:T(8,128)}, f32[448,512]{1,0:T(8,128)}, f32[1,224,384]{2,1,0:T(8,128)}) async-done(((f32[1,224,384]{2,1,0:T(8,128)}, f32[448,512]{1,0:T(8,128)}, f32[448,512]{1,0:T(8,128)}, f32[1,224,384]{2,1,0:T(8,128)}), (f32[1,224,384]{2,1,0:T(8,128)}, f32[448,512]{1,0:T(8,128)}, f32[448,512]{1,0:T(8,128)}, ...) | async-done | bytes 2523152 | tf_op jit(solution)/shard_map/psum | solution.py:109
  175.8 1.2 fusion.26
  177.0 0.7 copy-done.3
  177.6 3.4 convolution_multiply_fusion
  181.1 4.7 reshape.220
  185.7 5.7 %convolution_bitcast_fusion = f32[512,2048]{1,0:T(8,128)} fusion(f32[64,6,2048]{2,1,0:T(8,128)} %reshape.220, s32[64,8]{1,0:T(8,128)S(1)} %sub.15, pred[64,8]{1,0:T(8,128)(4,1)S(1)} %broadcast_compare_fusion), kind=kOutput, calls=%fused_computation.1 | convolution fusion | flops 75503616 | bytes 7342592 | tf_op jit(solution)/shard_map/kbmr,kbmd->brd/dot_general | solution.py:38
  191.4 3.3 fusion.19
  194.7 0.0 all-reduce.10.cloned.1.call-update
  194.7 0.0 all-gather.5.cloned.1.call-start
  194.8 0.6 copy-done.15
  195.4 0.6 dynamic-slice
  196.6 202.0 %all-reduce.10.cloned.1.call-done = (f32[512,2048]{1,0:T(8,128)}, f32[512,2048]{1,0:T(8,128)}) async-done(((f32[512,2048]{1,0:T(8,128)}, f32[512,2048]{1,0:T(8,128)}), (f32[512,2048]{1,0:T(8,128)}, f32[512,2048]{1,0:T(8,128)})) %all-reduce.10.cloned.1.call-update) | async-done | bytes 8388624
  398.6 1.5 fusion.38
  400.1 0.0 all-gather.5.cloned.1.call-update
  400.1 0.2 all-reduce.8.cloned.1.call-start
  400.4 79.4 %all-gather.5.cloned.1.call-done = bf16[512,2048]{1,0:T(8,128)(2,1)} async-done(((bf16[8,2048]{1,0:T(8,128)(2,1)}), bf16[512,2048]{1,0:T(8,128)(2,1)}) %all-gather.5.cloned.1.call-update) | async-done | bytes 2097168 | tf_op jit(solution)/shard_map/all_gather | solution.py:45
  479.7 4.2 convert_bitcast_fusion
  484.0 6.4 %reshape.226 = f32[1,384,1,1,1,1,2048]{6,0,1,5,4,3,2:T(1,128)} reshape(f32[1,64,6,2048]{3,2,1,0:T(8,128)} %convert_bitcast_fusion) | data formatting | bytes 6291456 | tf_op jit(solution)/shard_map/convert_element_type | solution.py:134
  490.4 4.2 multiply_convert_fusion
  494.6 1.6 copy-done.1
  496.3 1.9 fusion.10
  498.2 0.0 all-reduce.8.cloned.1.call-update
  498.2 4.1 fusion.4
  502.3 38.3 %all-reduce.8.cloned.1.call-done = f32[1,224,384]{2,1,0:T(8,128)} async-done(((f32[1,224,384]{2,1,0:T(8,128)}), f32[1,224,384]{2,1,0:T(8,128)}) %all-reduce.8.cloned.1.call-update) | async-done | bytes 344080 | tf_op jit(solution)/shard_map/psum | solution.py:142
  540.7 2.8 fusion.3
  543.4 1.6 fusion.2
  (29 shorter events, 0.1 us)
Async XLA Ops:
  7.2 184.3 %copy-start = (bf16[448,2048]{1,0:T(8,128)(2,1)S(1)}, bf16[448,2048]{1,0:T(8,128)(2,1)}, u32[]{:S(2)}) copy-start(bf16[448,2048]{1,0:T(8,128)(2,1)} %param.12) | copy-start | bytes 5505028
  7.2 85.2 %all-gather.3.cloned.1.call-start = ((), (), s32[]{:S(2)}) async-start(), calls=%async_computation | async-start | bytes 2129920 | tf_op jit(solution)/shard_map/all_gather | solution.py:75
  7.9 167.9 %all-reduce.12.cloned.1.call-start = ((), (), s32[]{:S(2)}) async-start(), calls=%async_computation.4 | async-start | bytes 5046272 | tf_op jit(solution)/shard_map/psum | solution.py:109
  98.6 2.8 copy-start.4
  98.6 4.2 copy-start.10
  101.4 1.6 copy-start.2
  103.0 2.1 copy-start.11
  107.1 0.7 copy-start.8
  107.1 0.7 copy-start.9
  107.1 291.5 %all-reduce.10.cloned.1.call-start = ((), (), s32[]{:S(2)}) async-start(), calls=%async_computation.3 | async-start | bytes 16777216
  177.0 0.7 copy-start.3
  185.7 5.7 %copy-start.12 = (f32[448,512]{1,0:T(8,128)S(1)}, f32[448,512]{1,0:T(8,128)}, u32[]{:S(2)}) copy-start(f32[448,512]{1,0:T(8,128)} %get-tuple-element.6) | copy-start | bytes 2752516
  185.7 5.7 %copy-start.13 = (f32[448,512]{1,0:T(8,128)S(1)}, f32[448,512]{1,0:T(8,128)}, u32[]{:S(2)}) copy-start(f32[448,512]{1,0:T(8,128)} %get-tuple-element.7) | copy-start | bytes 2752516
  194.7 0.7 copy-start.15
  194.7 285.0 %all-gather.5.cloned.1.call-start = ((), (), s32[]{:S(2)}) async-start(), calls=%async_computation.1 | async-start | bytes 2129920 | tf_op jit(solution)/shard_map/all_gather | solution.py:45
  400.1 140.5 %all-reduce.8.cloned.1.call-start = ((), (), s32[]{:S(2)}) async-start(), calls=%async_computation.2 | async-start | bytes 688128 | tf_op jit(solution)/shard_map/psum | solution.py:142
  490.4 5.9 %copy-start.5 = (bf16[1,224,2048]{2,1,0:T(8,128)(2,1)S(1)}, bf16[1,224,2048]{2,1,0:T(8,128)(2,1)}, u32[]{:S(2)}) copy-start(bf16[1,224,2048]{2,1,0:T(8,128)(2,1)} %param.15) | copy-start | bytes 2752516
  494.6 1.7 copy-start.1
  540.7 2.8 copy-start.6
  540.7 2.8 copy-start.7
  540.7 2.8 copy-start.14
Sparse Core Ops, SparseCore 0:
  10.8 81.5 all-gather.2
  107.2 68.4 all-reduce.11
  194.9 203.6 all-reduce.9
  401.8 77.8 all-gather.4
  498.4 42.2 all-reduce.7
where the time goes:
time: 553 us; the launch traced here: 552 us
  waiting for transfers between devices  471 us (85%)
  matrix products  39.4 us (7%)
  local copies, waits for them, and re-layouts  18.3 us (3%)
  between operations  14.6 us (3%)
  other arithmetic  7.83 us (1%)
    unnamed x6, waiting for transfers between devices  203 us
    all_gather x1, waiting for transfers between devices, body(): gathered = lax.all_gather(tokens, ('neuron', 'expert'), axis=0, tiled=True)  83.4 us
    all_gather x1, waiting for transfers between devices, spread_residual(): lax.all_gather(residual, ('neuron', 'expert'), axis=0, tiled=True)  79.4 us
    psum x1, waiting for transfers between devices, body(): expert_pre, expert_lift = lax.psum((pre_part, lift_part), 'dp')  67.3 us
    psum x1, waiting for transfers between devices, body(): hidden_total = lax.psum(hidden_part, 'dp')  38.3 us
  transfers between devices with their start and end apart: 5, of which 5 were waited for; matrix products, arithmetic and copies ran while one was open for 1% of the time, Pallas kernels for 0%

commit v1 on v0

v1 whole, which is shorter than its diff:
```python
import jax
import jax.numpy as jnp
from jax import lax
from jax.experimental import pallas as pl
from jax.experimental.pallas import tpu as pltpu
from jax.sharding import PartitionSpec as P

MESH = pl.DeviceIdType.MESH
F32, BF16 = jnp.float32, jnp.bfloat16
NX, NY, NZ = 4, 4, 8
ROWS = 16
WIDTH, HALF = 2048, 1024
TEACH, STUD = 448, 224
TQ, SQ = 112, 64
HQ = TQ + SQ
CHUNK = 256
ORDER = (0, 1, 7, 2, 6, 3, 5, 4)
POS = tuple(ORDER.index(k) for k in range(NZ))
PC = 256
ZSEND = (7, 1, 6, 2, 5, 3, 4)
NSEM = 160
NT = (((1,), (1,)), ((), ()))


def dot(a, b, dims=(((1,), (0,)), ((), ()))):
    return lax.dot_general(a, b, dims, preferred_element_type=F32)


def kernel(
    tokens, mix, tgate, tup, tdown, sgate, sup, sdown,
    ggate, gup, gdown,
    w1, wd, tok, res, tf, blk, psend, prec, pown, hall, spre, slift,
    fcore, rcore, facc, fsend, rz, ry, qsend, rqz, ysend, rpy,
    isend, irec, iown, grads, lsem, ssem, rsem,
):
    ix, iz, ie = lax.axis_index("dp"), lax.axis_index("neuron"), lax.axis_index("expert")
    iy, ic = ie // 2, lax.rem(ie, 2)
    oc = 1 - ic

    def dev(x=0, y=0, z=0, c=0):
        core = oc if c else ic
        return (lax.rem(ix + x, NX), lax.rem(iz + z, NZ), lax.rem(iy + y, NY) * 2 + core)

    partners = (
        [dev(x=k) for k in range(1, NX)] + [dev(y=k) for k in range(1, NY)]
        + [dev(z=k) for k in range(1, NZ)] + [dev(c=1)]
    )
    barrier = pltpu.get_barrier_semaphore()
    for p in partners:
        pl.semaphore_signal(barrier, inc=1, device_id=p, device_id_type=MESH)

    loads = []

    def load(src, dst):
        cp = pltpu.make_async_copy(src, dst, lsem.at[len(loads)])
        cp.start()
        loads.append(cp)

    zero = jnp.zeros((SQ // 2, WIDTH), BF16)
    w1[3, TQ + 32:HQ] = zero
    w1[3, HQ + TQ + 32:] = zero
    for h in range(2):
        wd[h, 3, TQ + 32:HQ] = jnp.zeros((SQ // 2, HALF), BF16)
    for j in range(NX):
        n = SQ if j < 3 else SQ // 2
        load(tgate.at[pl.ds(j * TQ, TQ)], w1.at[j, pl.ds(0, TQ)])
        load(sgate.at[0, pl.ds(j * SQ, n)], w1.at[j, pl.ds(TQ, n)])
        load(tup.at[pl.ds(j * TQ, TQ)], w1.at[j, pl.ds(HQ, TQ)])
        load(sup.at[0, pl.ds(j * SQ, n)], w1.at[j, pl.ds(HQ + TQ, n)])
    n_w1 = len(loads)
    for j in range(NX):
        n = SQ if j < 3 else SQ // 2
        for h in range(2):
            cols = pl.ds(h * HALF, HALF)
            load(tdown.at[pl.ds(j * TQ, TQ), cols], wd.at[h, j, pl.ds(0, TQ)])
            load(sdown.at[0, pl.ds(j * SQ, n), cols], wd.at[h, j, pl.ds(TQ, n)])

    for h in range(2):
        tf[h] = tokens[:, h * HALF:(h + 1) * HALF].astype(F32)
    blk[pl.ds(pl.multiple_of(ic * 8, 8), 8), :] = tf[ic]
    pl.semaphore_wait(barrier, len(partners))

    sent = []

    def send(src, dst, to):
        i = len(sent)
        cp = pltpu.make_async_remote_copy(
            src_ref=src, dst_ref=dst, send_sem=ssem.at[i], recv_sem=rsem.at[i],
            device_id=to, device_id_type=MESH,
        )
        cp.start()
        sent.append(cp)
        return cp

    cp = send(tf.at[oc], blk.at[pl.ds(pl.multiple_of(ic * 8, 8), 8), :], dev(c=1))
    cp.wait_recv()
    tok[ic, 0, 0:ROWS] = blk[...].astype(BF16)

    pcols, qcols = pl.ds(0, PC), pl.ds(PC, HALF - PC)

    def rows(k):
        return pl.ds((k % NY) * ROWS, ROWS)

    def gather_start(buf):
        own = buf.at[ic, 0, pl.ds(0, ROWS)]
        p1 = [send(own.at[:, pcols], buf.at[ic, 0, rows(-k), pcols], dev(y=k)) for k in (2, 1, 3)]
        q1 = {k: send(own.at[:, qcols], buf.at[ic, POS[-k % NZ], pl.ds(0, ROWS), qcols], dev(z=k))
              for k in ZSEND}
        for c in p1:
            c.wait_recv()
        p2 = {k: send(buf.at[ic, 0, :, pcols], buf.at[ic, POS[-k % NZ], :, pcols], dev(z=k))
              for k in ZSEND}
        return q1, p2

    def gather_spread(buf, q1, half):
        for k in (ZSEND[:3] if half == 0 else ZSEND[3:]):
            q1[k].wait_recv()
        group = pl.ds(half * 4, 4)
        return [send(buf.at[ic, group, pl.ds(0, ROWS), qcols], buf.at[ic, group, rows(-k), qcols], dev(y=k))
                for k in (2, 1, 3)]

    def gather_core(buf, p2, q2, half):
        for k in (ZSEND[:3] if half == 0 else ZSEND[3:]):
            p2[k].wait_recv()
        for c in q2:
            c.wait_recv()
        group = pl.ds(half * 4, 4)
        return send(buf.at[ic, group], buf.at[ic, group], dev(c=1))

    q1, p2 = gather_start(tok)
    q2a = gather_spread(tok, q1, 0)
    core_a = gather_core(tok, p2, q2a, 0)
    q2b = gather_spread(tok, q1, 1)
    for cp in loads[:n_w1]:
        cp.wait()
    core_a.wait_recv()

    def piece(buf, h, half):
        return buf[h, half * 4:half * 4 + 4].reshape(CHUNK, HALF)

    def hidden_parts(half):
        out = []
        for d in (2, 1, 3, 0):
            j = lax.rem(ix + d, NX)
            part = dot(w1[j, :, :HALF], piece(tok, 0, half), NT) + dot(w1[j, :, HALF:], piece(tok, 1, half), NT)
            if d == 0:
                pown[half] = part
            else:
                psend[half, d] = part.astype(BF16)
                out.append(send(psend.at[half, d], prec.at[half, NX - d], dev(x=d)))
        return out

    def activate(half, cps):
        for c in cps:
            c.wait_recv()
        total = pown[half]
        for d in range(1, NX):
            total = total + prec[half, d].astype(F32)
        pre, lift = total[:HQ], total[HQ:]
        cols = pl.ds(half * CHUNK, CHUNK)
        spre[:, cols] = pre[TQ:]
        slift[:, cols] = lift[TQ:]
        act = pre * jax.nn.sigmoid(pre) * lift
        hall[half, ix, 0:TQ] = (-act[:TQ]).astype(BF16)
        hall[half, ix, TQ:HQ] = (act[TQ:] * mix[:, cols]).astype(BF16)
        mine = hall.at[half, ix]
        return [send(mine, mine, dev(x=d)) for d in (2, 1, 3)]

    def outputs(half, cps):
        for c in cps:
            c.wait_recv()
        hidden = hall[half].reshape(NX * HQ, CHUNK).T
        fcore[half] = dot(hidden, wd[oc].reshape(NX * HQ, HALF)).astype(BF16)
        cp = send(fcore.at[half], rcore.at[half], dev(c=1))
        facc[half] = dot(hidden, wd[ic].reshape(NX * HQ, HALF))
        return cp

    def scatter_first(half, cp):
        cp.wait_recv()
        total = facc[half] + rcore[half].astype(F32)
        facc[half] = total
        fsend[half * 4:half * 4 + 4] = total.astype(BF16).reshape(4, 64, HALF)
        q = [send(fsend.at[pl.ds(half * 4, 4), rows(k), qcols], ry.at[half, NY - k], dev(y=k)) for k in (2, 1, 3)]
        p = []
        for pos in range(half * 4, half * 4 + 4):
            k = ORDER[pos]
            if k:
                p.append(send(fsend.at[pos, :, pcols], rz.at[POS[-k % NZ]], dev(z=k)))
        return q, p

    def scatter_second(half, q):
        for c in q:
            c.wait_recv()
        total = facc[half].reshape(4, 64, HALF)[:, :ROWS, PC:]
        for d in range(1, NY):
            total = total + ry[half, d].astype(F32)
        if half == 0:
            ysend[0:ROWS, PC:] = total[0]
        qsend[half * 4:half * 4 + 4] = total.astype(BF16)
        out = []
        for pos in range(half * 4, half * 4 + 4):
            k = ORDER[pos]
            if k:
                out.append(send(qsend.at[pos], rqz.at[POS[-k % NZ]], dev(z=k)))
        return out

    c0 = hidden_parts(0)
    core_b = gather_core(tok, p2, q2b, 1)
    core_b.wait_recv()
    c1 = hidden_parts(1)
    d0 = activate(0, c0)
    for cp in loads[n_w1:]:
        cp.wait()
    e0 = outputs(0, d0)
    f0q, f0p = scatter_first(0, e0)
    d1 = activate(1, c1)
    g0 = scatter_second(0, f0q)
    e1 = outputs(1, d1)
    f1q, f1p = scatter_first(1, e1)
    g1 = scatter_second(1, f1q)

    for c in f0p + f1p:
        c.wait_recv()
    total = facc[0, 0:64, :PC]
    for pos in range(1, NZ):
        total = total + rz[pos].astype(F32)
    ysend[:, :PC] = total
    qy = rpy.at[0]
    qy[...] = total.astype(BF16)
    hs = [send(rpy.at[0, rows(k)], rpy.at[NY - k, pl.ds(0, ROWS)], dev(y=k)) for k in (2, 1, 3)]
    for c in g0 + g1:
        c.wait_recv()
    total = ysend[0:ROWS, PC:]
    for pos in range(1, NZ):
        total = total + rqz[pos].astype(F32)
    res[ic, 0, 0:ROWS, PC:] = total.astype(BF16)
    for c in hs:
        c.wait_recv()
    total = ysend[0:ROWS, :PC]
    for d in range(1, NY):
        total = total + rpy[d, 0:ROWS].astype(F32)
    res[ic, 0, 0:ROWS, :PC] = total.astype(BF16)

    q1, p2 = gather_start(res)
    q2a = gather_spread(res, q1, 0)
    core_a = gather_core(res, p2, q2a, 0)
    q2b = gather_spread(res, q1, 1)
    core_a.wait_recv()

    def hidden_grads(half):
        out = []
        for d in (2, 1, 3, 0):
            j = lax.rem(ix + d, NX)
            part = dot(wd[0, j, TQ:], piece(res, 0, half), NT) + dot(wd[1, j, TQ:], piece(res, 1, half), NT)
            if d == 0:
                iown[half] = part
            else:
                isend[half, d] = part.astype(BF16)
                out.append(send(isend.at[half, d], irec.at[half, NX - d], dev(x=d)))
        return out

    def slopes(half, cps):
        for c in cps:
            c.wait_recv()
        total = iown[half]
        for d in range(1, NX):
            total = total + irec[half, d].astype(F32)
        cols = pl.ds(half * CHUNK, CHUNK)
        total = total * mix[:, cols]
        pre, lift = spre[:, cols], slift[:, cols]
        s = jax.nn.sigmoid(pre)
        grads[half, 0, ix] = (total * lift * (s * (1.0 + pre * (1.0 - s)))).astype(BF16)
        grads[half, 1, ix] = (total * (pre * s)).astype(BF16)
        mine = grads.at[half, :, ix]
        return [send(mine, mine, dev(x=d)) for d in (2, 1, 3)]

    i0 = hidden_grads(0)
    core_b = gather_core(res, p2, q2b, 1)
    core_b.wait_recv()
    i1 = hidden_grads(1)
    j0 = slopes(0, i0)

    def product(left, buf, h):
        return dot(left[0], piece(buf, h, 0)) + dot(left[1], piece(buf, h, 1))

    hm = [hall[half, :, TQ:].reshape(NX * SQ, CHUNK) for half in range(2)]
    for h in range(2):
        gdown[0, :, h * HALF:(h + 1) * HALF] = product(hm, res, h)[:STUD].astype(BF16)
    j1 = slopes(1, i1)
    for c in j0 + j1:
        c.wait_recv()
    for n, out in enumerate((ggate, gup)):
        left = [grads[half, n].reshape(NX * SQ, CHUNK) for half in range(2)]
        for h in range(2):
            out[0, :, h * HALF:(h + 1) * HALF] = product(left, tok, h)[:STUD].astype(BF16)
    for c in sent:
        c.wait_send()


def body(tokens, tgate, tup, tdown, sgate, sup, sdown, routes, route_weight):
    iz, ie = lax.axis_index("neuron"), lax.axis_index("expert")
    mixing = jnp.sum(jnp.where(routes == ie, route_weight, 0.0), axis=1).reshape(NZ, NY, ROWS)
    zs = lax.rem(iz + jnp.array(ORDER, jnp.int32), NZ)
    ys = lax.rem(ie // 2 + jnp.arange(NY, dtype=jnp.int32), NY)
    mix = mixing[zs][:, ys].reshape(1, NZ * NY * ROWS)
    vmem, anym = pl.BlockSpec(memory_space=pltpu.VMEM), pl.BlockSpec(memory_space=pl.ANY)
    grad = jax.ShapeDtypeStruct((1, STUD, WIDTH), BF16)
    V = pltpu.VMEM
    return pl.pallas_call(
        kernel,
        out_shape=(grad, grad, grad),
        in_specs=[vmem, vmem] + [anym] * 6,
        out_specs=(vmem, vmem, vmem),
        scratch_shapes=[
            V((NX, 2 * HQ, WIDTH), BF16),
            V((2, NX, HQ, HALF), BF16),
            V((2, NZ, 64, HALF), BF16),
            V((2, NZ, 64, HALF), BF16),
            V((2, 8, HALF), F32),
            V((ROWS, HALF), F32),
            V((2, NX, 2 * HQ, CHUNK), BF16),
            V((2, NX, 2 * HQ, CHUNK), BF16),
            V((2, 2 * HQ, CHUNK), F32),
            V((2, NX, HQ, CHUNK), BF16),
            V((SQ, 2 * CHUNK), F32),
            V((SQ, 2 * CHUNK), F32),
            V((2, CHUNK, HALF), BF16),
            V((2, CHUNK, HALF), BF16),
            V((2, CHUNK, HALF), F32),
            V((NZ, 64, HALF), BF16),
            V((NZ, 64, PC), BF16),
            V((2, NY, 4, ROWS, HALF - PC), BF16),
            V((NZ, ROWS, HALF - PC), BF16),
            V((NZ, ROWS, HALF - PC), BF16),
            V((64, HALF), F32),
            V((NY, 64, PC), BF16),
            V((2, NX, SQ, CHUNK), BF16),
            V((2, NX, SQ, CHUNK), BF16),
            V((2, SQ, CHUNK), F32),
            V((2, 2, NX, SQ, CHUNK), BF16),
            pltpu.SemaphoreType.DMA((32,)),
            pltpu.SemaphoreType.DMA((NSEM,)),
            pltpu.SemaphoreType.DMA((NSEM,)),
        ],
        compiler_params=pltpu.CompilerParams(
            collective_id=0, has_side_effects=True, vmem_limit_bytes=56 * 2**20
        ),
        cost_estimate=pl.CostEstimate(flops=6 * 10**9, bytes_accessed=12 * 10**6, transcendentals=10**6),
        name="distill",
    )(tokens, mix, tgate, tup, tdown, sgate, sup, sdown)


def solution(mesh):
    split = P(("neuron", "expert"), "dp")
    expert = P("expert", "neuron", "dp")
    return jax.shard_map(
        body,
        mesh=mesh,
        in_specs=(split, split, split, split, expert, expert, expert, P(), P()),
        out_specs=(expert, expert, expert),
        check_vma=False,
    )
```

time: 553 us -> 114 us (0.21)
  waiting for transfers between devices: 471 us -> 0 us
  Pallas kernels: 0 us -> 106 us
  matrix products: 39.4 us -> 0 us
  between operations: 14.6 us -> 0.71 us
  local copies, waits for them, and re-layouts: 18.3 us -> 6.08 us
  other arithmetic: 7.83 us -> 1.41 us
    unnamed x6 -> x0, waiting for transfers between devices: 203 us -> none
    all_gather x2 -> x0, waiting for transfers between devices: 163 us -> none  [the longest x1 83.4 us: body(): gathered = lax.all_gather(tokens, ('neuron', 'expert'), axis=0, tiled=True)]
    pallas_call x0 -> x1, Pallas kernels: none -> 106 us  [body(): pl.pallas_call(kernel, out_shape=(grad, grad, grad), in_specs=[vmem, vmem...]
    psum x2 -> x0, waiting for transfers between devices: 106 us -> none  [the longest x1 67.3 us: body(): expert_pre, expert_lift = lax.psum((pre_part, lift_part), 'dp')]
    dot_general x14 -> x0, matrix products: 39.4 us -> none  [the longest x1 5.71 us: student_term(): jnp.einsum('kbmr,kbmd->brd', selector, weighted_blocks, precision=lax.Pre...]
    another operation x3 -> x0, local copies, waits for them, and re-layouts: 7.34 us -> none
    convert_element_type x2 -> x0, local copies, waits for them, and re-layouts: 6.5 us -> none  [the longest x1 6.42 us: body(): slot_residual.astype(jnp.float32) * slot_mixing[:, :, None]]
    convert_element_type x3 -> x0, other arithmetic: 5.73 us -> none  [the longest x1 4.23 us: body(): (slot_residual.astype(jnp.float32) * slot_mixing[:, :, None]).astype(jnp....]
  transfers between devices with their start and end apart: 5 -> 0, of which waited for: 5 -> 0; matrix products, arithmetic and copies ran while one was open for 1% -> 0% of each run, Pallas kernels for 0% -> 0%
where the time goes in v1:
time: 114 us
  Pallas kernels  106 us (93%)
  local copies, waits for them, and re-layouts  6.08 us (5%)
  other arithmetic  1.41 us (1%)
    pallas_call x1, Pallas kernels, body(): pl.pallas_call(kernel, out_shape=(grad, grad, grad), in_specs=[vmem, vmem...  106 us
    unnamed x7, local copies, waits for them, and re-layouts  4.18 us

profile of v1, /device:TPU:1, one launch (start us, length us, event | category | flops | bytes accessed | tf_op | source)
XLA Modules:
  0.0 114.2 jit_solution(12747583613796883880)
XLA Ops:
  0.7 0.7 compare_select_fusion.2
  1.3 0.7 fusion
  2.1 0.1 reshape.46
  2.2 0.6 gather_fusion
  2.7 0.6 gather_fusion.1
  3.3 0.7 reshape.47.mix
  4.0 106.0 %distill.1 = (bf16[1,224,2048]{2,1,0:T(8,128)(2,1)}, bf16[1,224,2048]{2,1,0:T(8,128)(2,1)}, bf16[1,224,2048]{2,1,0:T(8,128)(2,1)}) custom-call(bf16[8,2048]{1,0:T(8,128)(2,1)} %tokens.1, f32[1,512]{1,0:T(1,128)} %reshape.47.mix, bf16[448,2048]{1,0:T(8,128)(2,1)} %tgate.1, bf16[448,2048]{1,0:T(8,128)(2,1)} %tup.1, bf16[448,2048]{1,0:T(8,128)(2,1)} %tdown.1, ...), custom_call_target="tpu_custom_call" | custom-call | flops 6000000000 | bytes 12000000 | tf_op jit(solution)/shard_map/distill/pallas_call | solution.py:309
  110.0 0.0 copy-start.1
  110.0 0.0 copy-start
  110.0 2.3 %copy.19 = bf16[1,224,2048]{2,1,0:T(8,128)(2,1)} copy(bf16[1,224,2048]{2,1,0:T(8,128)(2,1)} %get-tuple-element.6) | data formatting | bytes 1835008
  112.4 0.0 copy-done.1
  112.4 0.9 copy.20
  113.3 0.0 copy-done
  113.3 0.9 copy.21
  (5 shorter events, 0.0 us)
Async XLA Ops:
  110.0 2.4 %copy-start.1 = (bf16[1,224,2048]{2,1,0:T(8,128)(2,1)S(1)}, bf16[1,224,2048]{2,1,0:T(8,128)(2,1)}, u32[]{:S(2)}) copy-start(bf16[1,224,2048]{2,1,0:T(8,128)(2,1)} %get-tuple-element.7) | copy-start | bytes 2752516
  110.0 3.3 %copy-start = (bf16[1,224,2048]{2,1,0:T(8,128)(2,1)S(1)}, bf16[1,224,2048]{2,1,0:T(8,128)(2,1)}, u32[]{:S(2)}) copy-start(bf16[1,224,2048]{2,1,0:T(8,128)(2,1)} %get-tuple-element.8) | copy-start | bytes 2752516

commit v2 on v1

v2 whole, which is shorter than its diff:
```python
import jax
import jax.numpy as jnp
from jax import lax
from jax.experimental import pallas as pl
from jax.experimental.pallas import tpu as pltpu
from jax.sharding import PartitionSpec as P

MESH = pl.DeviceIdType.MESH
F32, BF16 = jnp.float32, jnp.bfloat16
NX, NY, NZ = 4, 4, 8
ROWS = 16
WIDTH, HALF = 2048, 1024
TEACH, STUD = 448, 224
TQ, SQ = 112, 64
HQ = TQ + SQ
CHUNK, PARTS, SLABS = 128, 4, 2
TOKENS = CHUNK * PARTS
ORDER = (0, 1, 7, 2, 6, 3, 5, 4)
POS = tuple(ORDER.index(k) for k in range(NZ))
PC = 256
ZSEND = ((7,), (1, 6), (2, 5), (3, 4))
NSEM = 176
NT = (((1,), (1,)), ((), ()))


def dot(a, b, dims=(((1,), (0,)), ((), ()))):
    return lax.dot_general(a, b, dims, preferred_element_type=F32)


def kernel(
    tokens, routes, weights, tgate, tup, tdown, sgate, sup, sdown,
    tok, res, pgrad, lgrad, hm,
    w1, wd, tf, blk, mix, psend, prec, pown, hall, fac,
    fcore, rcore, facc, fsend, rz, ry, qsend, rqz, ysend, rpy,
    isend, irec, iown, hgrad, lsem, ssem, rsem,
):
    ix, iz, ie = lax.axis_index("dp"), lax.axis_index("neuron"), lax.axis_index("expert")
    iy, ic = ie // 2, lax.rem(ie, 2)
    oc = 1 - ic

    def dev(x=0, y=0, z=0, c=0):
        core = oc if c else ic
        return (lax.rem(ix + x, NX), lax.rem(iz + z, NZ), lax.rem(iy + y, NY) * 2 + core)

    partners = (
        [dev(x=k) for k in range(1, NX)] + [dev(y=k) for k in range(1, NY)]
        + [dev(z=k) for k in range(1, NZ)] + [dev(c=1)]
    )
    barrier = pltpu.get_barrier_semaphore()
    for p in partners:
        pl.semaphore_signal(barrier, inc=1, device_id=p, device_id_type=MESH)

    loads = []

    def load(src, dst):
        cp = pltpu.make_async_copy(src, dst, lsem.at[len(loads)])
        cp.start()
        loads.append(cp)

    zero = jnp.zeros((SQ // 2, WIDTH), BF16)
    w1[3, TQ + 32:HQ] = zero
    w1[3, HQ + TQ + 32:] = zero
    for h in range(2):
        wd[h, 3, TQ + 32:HQ] = jnp.zeros((SQ // 2, HALF), BF16)
    for j in range(NX):
        n = SQ if j < 3 else SQ // 2
        load(tgate.at[pl.ds(j * TQ, TQ)], w1.at[j, pl.ds(0, TQ)])
        load(sgate.at[0, pl.ds(j * SQ, n)], w1.at[j, pl.ds(TQ, n)])
        load(tup.at[pl.ds(j * TQ, TQ)], w1.at[j, pl.ds(HQ, TQ)])
        load(sup.at[0, pl.ds(j * SQ, n)], w1.at[j, pl.ds(HQ + TQ, n)])
    n_w1 = len(loads)
    for j in range(NX):
        n = SQ if j < 3 else SQ // 2
        for h in range(2):
            cols = pl.ds(h * HALF, HALF)
            load(tdown.at[pl.ds(j * TQ, TQ), cols], wd.at[h, j, pl.ds(0, TQ)])
            load(sdown.at[0, pl.ds(j * SQ, n), cols], wd.at[h, j, pl.ds(TQ, n)])

    for h in range(2):
        tf[h] = tokens[:, h * HALF:(h + 1) * HALF].astype(F32)
    blk[pl.ds(pl.multiple_of(ic * 8, 8), 8), :] = tf[ic]
    pl.semaphore_wait(barrier, len(partners))

    sent = []

    def send(src, dst, to):
        i = len(sent)
        cp = pltpu.make_async_remote_copy(
            src_ref=src, dst_ref=dst, send_sem=ssem.at[i], recv_sem=rsem.at[i],
            device_id=to, device_id_type=MESH,
        )
        cp.start()
        sent.append(cp)
        return cp

    def arrived(cps):
        for c in cps:
            c.wait_recv()

    cp = send(tf.at[oc], blk.at[pl.ds(pl.multiple_of(ic * 8, 8), 8), :], dev(c=1))
    cp.wait_recv()
    tok[ic, 0, 0:ROWS] = blk[...].astype(BF16)

    pcols, qcols = pl.ds(0, PC), pl.ds(PC, HALF - PC)

    def rows(k):
        return pl.ds((k % NY) * ROWS, ROWS)

    def group(part):
        return pl.ds(part * SLABS, SLABS)

    def gather_start(buf):
        own = buf.at[ic, 0, pl.ds(0, ROWS)]
        p1 = [send(own.at[:, pcols], buf.at[ic, 0, rows(-k), pcols], dev(y=k)) for k in (2, 1, 3)]
        q1 = [[send(own.at[:, qcols], buf.at[ic, POS[-k % NZ], pl.ds(0, ROWS), qcols], dev(z=k)) for k in ks]
              for ks in ZSEND]
        arrived(p1)
        p2 = [[send(buf.at[ic, 0, :, pcols], buf.at[ic, POS[-k % NZ], :, pcols], dev(z=k)) for k in ks]
              for ks in ZSEND]
        return [q1, p2, [None] * PARTS, [None] * PARTS]

    def spread(buf, state, part):
        arrived(state[0][part])
        g = group(part)
        state[2][part] = [
            send(buf.at[ic, g, pl.ds(0, ROWS), qcols], buf.at[ic, g, rows(-k), qcols], dev(y=k)) for k in (2, 1, 3)
        ]

    def to_core(buf, state, part):
        arrived(state[1][part])
        arrived(state[2][part])
        state[3][part] = send(buf.at[ic, group(part)], buf.at[ic, group(part)], dev(c=1))

    def piece(buf, h, part):
        return buf[h, part * SLABS:(part + 1) * SLABS].reshape(CHUNK, HALF)

    def hidden_parts(part):
        out = []
        for d in (2, 1, 3, 0):
            j = lax.rem(ix + d, NX)
            val = dot(w1[j, :, :HALF], piece(tok, 0, part), NT) + dot(w1[j, :, HALF:], piece(tok, 1, part), NT)
            if d == 0:
                pown[part] = val
            else:
                psend[part, d] = val.astype(BF16)
                out.append(send(psend.at[part, d], prec.at[part, NX - d], dev(x=d)))
        return out

    def activate(part, cps):
        arrived(cps)
        total = pown[part]
        for d in range(1, NX):
            total = total + prec[part, d].astype(F32)
        pre, lift = total[:HQ], total[HQ:]
        s = jax.nn.sigmoid(pre)
        act = pre * s
        hidden = act * lift
        weight = mix[part, 0:1]
        hall[part, ix, 0:TQ] = (-hidden[:TQ]).astype(BF16)
        hall[part, ix, TQ:HQ] = (hidden[TQ:] * weight).astype(BF16)
        mine = hall.at[part, ix]
        out = [send(mine, mine, dev(x=d)) for d in (2, 1, 3)]
        slope = s * (1.0 + pre * (1.0 - s))
        fac[ix, part, 0] = (weight * (lift * slope)[TQ:]).astype(BF16)
        fac[ix, part, 1] = (weight * act[TQ:]).astype(BF16)
        return out

    def outputs(part, cps):
        arrived(cps)
        hidden = hall[part].reshape(NX * HQ, CHUNK).T
        fcore[part] = dot(hidden, wd[oc].reshape(NX * HQ, HALF)).astype(BF16)
        cp = send(fcore.at[part], rcore.at[part], dev(c=1))
        facc[part] = dot(hidden, wd[ic].reshape(NX * HQ, HALF))
        return cp

    def scatter_first(part, cp):
        cp.wait_recv()
        total = facc[part] + rcore[part].astype(F32)
        facc[part] = total
        fsend[part * SLABS:(part + 1) * SLABS] = total.astype(BF16).reshape(SLABS, 64, HALF)
        q = [send(fsend.at[group(part), rows(k), qcols], ry.at[part, NY - k], dev(y=k)) for k in (2, 1, 3)]
        p = []
        for pos in range(part * SLABS, (part + 1) * SLABS):
            k = ORDER[pos]
            if k:
                p.append(send(fsend.at[pos, :, pcols], rz.at[POS[-k % NZ]], dev(z=k)))
        return q, p

    def scatter_second(part, q):
        arrived(q)
        total = facc[part].reshape(SLABS, 64, HALF)[:, :ROWS, PC:]
        for d in range(1, NY):
            total = total + ry[part, d].astype(F32)
        if part == 0:
            ysend[0:ROWS, PC:] = total[0]
        qsend[part * SLABS:(part + 1) * SLABS] = total.astype(BF16)
        out = []
        for pos in range(part * SLABS, (part + 1) * SLABS):
            k = ORDER[pos]
            if k:
                out.append(send(qsend.at[pos], rqz.at[POS[-k % NZ]], dev(z=k)))
        return out

    def mixing():
        m = jnp.sum(jnp.where(routes[...] == ie, weights[...], 0.0), axis=0, keepdims=True)
        m = jnp.broadcast_to(m, (8, TOKENS))
        m = pltpu.roll(m, lax.rem(NZ - iz, NZ) * 64, 1)
        lane = lax.broadcasted_iota(jnp.int32, (8, TOKENS), 1)
        near = pltpu.roll(m, lax.rem(TOKENS - iy * ROWS, TOKENS), 1)
        far = pltpu.roll(m, 64 - iy * ROWS, 1)
        m = jnp.where(lax.rem(lane, 64) < 64 - iy * ROWS, near, far)
        low = lax.broadcasted_iota(jnp.int32, (8, CHUNK), 1) < 64
        for part in range(PARTS):
            two = []
            for side in range(2):
                k = ORDER[part * 2 + side]
                t = m[:, (k // 2) * CHUNK:(k // 2 + 1) * CHUNK]
                two.append(t if k % 2 == side else pltpu.roll(t, 64, 1))
            mix[part] = jnp.where(low, two[0], two[1])

    P4 = range(PARTS)
    c, d, e, q, p, g = ([None] * PARTS for _ in range(6))
    state = gather_start(tok)
    mixing()
    spread(tok, state, 0)
    spread(tok, state, 1)
    to_core(tok, state, 0)
    spread(tok, state, 2)
    for cp in loads[:n_w1]:
        cp.wait()
    state[3][0].wait_recv()
    c[0] = hidden_parts(0)
    to_core(tok, state, 1)
    spread(tok, state, 3)
    state[3][1].wait_recv()
    c[1] = hidden_parts(1)
    to_core(tok, state, 2)
    state[3][2].wait_recv()
    c[2] = hidden_parts(2)
    to_core(tok, state, 3)
    d[0] = activate(0, c[0])
    state[3][3].wait_recv()
    c[3] = hidden_parts(3)
    d[1] = activate(1, c[1])
    for cp in loads[n_w1:]:
        cp.wait()
    e[0] = outputs(0, d[0])
    d[2] = activate(2, c[2])
    q[0], p[0] = scatter_first(0, e[0])
    e[1] = outputs(1, d[1])
    d[3] = activate(3, c[3])
    factors = [send(fac.at[ix], fac.at[ix], dev(x=k)) for k in (2, 1, 3)]
    g[0] = scatter_second(0, q[0])
    q[1], p[1] = scatter_first(1, e[1])
    e[2] = outputs(2, d[2])
    g[1] = scatter_second(1, q[1])
    q[2], p[2] = scatter_first(2, e[2])
    e[3] = outputs(3, d[3])
    g[2] = scatter_second(2, q[2])
    q[3], p[3] = scatter_first(3, e[3])
    g[3] = scatter_second(3, q[3])

    total = facc[0, 0:64, :PC]
    for part in P4:
        arrived(p[part])
    for pos in range(1, NZ):
        total = total + rz[pos].astype(F32)
    ysend[:, :PC] = total
    rpy[0] = total.astype(BF16)
    hs = [send(rpy.at[0, rows(k)], rpy.at[NY - k, pl.ds(0, ROWS)], dev(y=k)) for k in (2, 1, 3)]
    for part in P4:
        arrived(g[part])
    total = ysend[0:ROWS, PC:]
    for pos in range(1, NZ):
        total = total + rqz[pos].astype(F32)
    res[ic, 0, 0:ROWS, PC:] = total.astype(BF16)
    arrived(hs)
    total = ysend[0:ROWS, :PC]
    for k in range(1, NY):
        total = total + rpy[k, 0:ROWS].astype(F32)
    res[ic, 0, 0:ROWS, :PC] = total.astype(BF16)

    def hidden_grads(part):
        out = []
        for d in (2, 1, 3, 0):
            j = lax.rem(ix + d, NX)
            val = dot(wd[0, j, TQ:], piece(res, 0, part), NT) + dot(wd[1, j, TQ:], piece(res, 1, part), NT)
            if d == 0:
                iown[part] = val
            else:
                isend[part, d] = val.astype(BF16)
                out.append(send(isend.at[part, d], irec.at[part, NX - d], dev(x=d)))
        return out

    def hidden_sum(part, cps):
        arrived(cps)
        total = iown[part]
        for d in range(1, NX):
            total = total + irec[part, d].astype(F32)
        hgrad[part, ix] = total.astype(BF16)
        mine = hgrad.at[part, ix]
        return [send(mine, mine, dev(x=d)) for d in (2, 1, 3)]

    def slopes(part, cps):
        arrived(cps)
        cols = pl.ds(part * CHUNK, CHUNK)
        for j in range(NX):
            grad = hgrad[part, j].astype(F32)
            units = pl.ds(j * SQ, SQ)
            pgrad[units, cols] = (grad * fac[j, part, 0].astype(F32)).astype(BF16)
            lgrad[units, cols] = (grad * fac[j, part, 1].astype(F32)).astype(BF16)

    state = gather_start(res)
    for part in P4:
        for j in range(NX):
            hm[j * SQ:(j + 1) * SQ, part * CHUNK:(part + 1) * CHUNK] = hall[part, j, TQ:HQ]
    spread(res, state, 0)
    spread(res, state, 1)
    to_core(res, state, 0)
    spread(res, state, 2)
    state[3][0].wait_recv()
    c[0] = hidden_grads(0)
    to_core(res, state, 1)
    spread(res, state, 3)
    state[3][1].wait_recv()
    c[1] = hidden_grads(1)
    to_core(res, state, 2)
    d[0] = hidden_sum(0, c[0])
    state[3][2].wait_recv()
    c[2] = hidden_grads(2)
    to_core(res, state, 3)
    d[1] = hidden_sum(1, c[1])
    state[3][3].wait_recv()
    c[3] = hidden_grads(3)
    d[2] = hidden_sum(2, c[2])
    arrived(factors)
    slopes(0, d[0])
    slopes(1, d[1])
    d[3] = hidden_sum(3, c[3])
    slopes(2, d[2])
    slopes(3, d[3])
    for cp in sent:
        cp.wait_send()


def products(tok, res, pgrad, lgrad, hm, ggate, gup, gdown, stage, sem):
    copies = []
    for n, (left, right, out) in enumerate(((hm, res, gdown), (pgrad, tok, ggate), (lgrad, tok, gup))):
        for h in range(2):
            val = dot(left[:STUD], right[h].reshape(TOKENS, HALF))
            stage[n, h] = val.astype(BF16)
            cp = pltpu.make_async_copy(stage.at[n, h], out.at[0, :, pl.ds(h * HALF, HALF)], sem.at[n, h])
            cp.start()
            copies.append(cp)
    for cp in copies:
        cp.wait()


def body(tokens, tgate, tup, tdown, sgate, sup, sdown, routes, route_weight):
    vmem, anym = pl.BlockSpec(memory_space=pltpu.VMEM), pl.BlockSpec(memory_space=pl.ANY)
    V = pltpu.VMEM
    held = (
        V((2, NZ, 64, HALF), BF16),
        V((2, NZ, 64, HALF), BF16),
        V((NX * SQ, TOKENS), BF16),
        V((NX * SQ, TOKENS), BF16),
        V((NX * SQ, TOKENS), BF16),
    )
    parts = pl.pallas_call(
        kernel,
        out_shape=held,
        in_specs=[vmem] * 3 + [anym] * 6,
        out_specs=(vmem,) * 5,
        scratch_shapes=[
            V((NX, 2 * HQ, WIDTH), BF16),
            V((2, NX, HQ, HALF), BF16),
            V((2, 8, HALF), F32),
            V((ROWS, HALF), F32),
            V((PARTS, 8, CHUNK), F32),
            V((PARTS, NX, 2 * HQ, CHUNK), BF16),
            V((PARTS, NX, 2 * HQ, CHUNK), BF16),
            V((PARTS, 2 * HQ, CHUNK), F32),
            V((PARTS, NX, HQ, CHUNK), BF16),
            V((NX, PARTS, 2, SQ, CHUNK), BF16),
            V((PARTS, CHUNK, HALF), BF16),
            V((PARTS, CHUNK, HALF), BF16),
            V((PARTS, CHUNK, HALF), F32),
            V((NZ, 64, HALF), BF16),
            V((NZ, 64, PC), BF16),
            V((PARTS, NY, SLABS, ROWS, HALF - PC), BF16),
            V((NZ, ROWS, HALF - PC), BF16),
            V((NZ, ROWS, HALF - PC), BF16),
            V((64, HALF), F32),
            V((NY, 64, PC), BF16),
            V((PARTS, NX, SQ, CHUNK), BF16),
            V((PARTS, NX, SQ, CHUNK), BF16),
            V((PARTS, SQ, CHUNK), F32),
            V((PARTS, NX, SQ, CHUNK), BF16),
            pltpu.SemaphoreType.DMA((32,)),
            pltpu.SemaphoreType.DMA((NSEM,)),
            pltpu.SemaphoreType.DMA((NSEM,)),
        ],
        compiler_params=pltpu.CompilerParams(
            collective_id=0, has_side_effects=True, vmem_limit_bytes=40 * 2**20
        ),
        cost_estimate=pl.CostEstimate(flops=6 * 10**9, bytes_accessed=12 * 10**6, transcendentals=10**6),
        name="distill",
    )(tokens, routes.T, route_weight.T, *(pltpu.with_memory_space_constraint(w, pltpu.HBM) for w in (tgate, tup, tdown, sgate, sup, sdown)))
    grad = jax.ShapeDtypeStruct((1, STUD, WIDTH), BF16)
    return pl.pallas_call(
        products,
        out_shape=(grad, grad, grad),
        in_specs=[vmem] * 5,
        out_specs=(anym,) * 3,
        scratch_shapes=[V((3, 2, STUD, HALF), BF16), pltpu.SemaphoreType.DMA((3, 2))],
        compiler_params=pltpu.CompilerParams(vmem_limit_bytes=16 * 2**20),
        cost_estimate=pl.CostEstimate(flops=15 * 10**8, bytes_accessed=3 * 10**6, transcendentals=0),
        name="products",
    )(*parts)


def solution(mesh):
    split = P(("neuron", "expert"), "dp")
    expert = P("expert", "neuron", "dp")
    return jax.shard_map(
        body,
        mesh=mesh,
        in_specs=(split, split, split, split, expert, expert, expert, P(), P()),
        out_specs=(expert, expert, expert),
        check_vma=False,
    )
```

time: 114 us -> 103 us (0.904)
  Pallas kernels: 106 us -> 99.3 us
  local copies, waits for them, and re-layouts: 6.08 us -> 2.12 us
  other arithmetic: 1.41 us -> 0 us
    pallas_call x1 -> x2, Pallas kernels: 106 us -> 99.3 us  [the longest x1 96.9 us: body(): pl.pallas_call(kernel, out_shape=held, in_specs=[vmem] * 3 + [anym] * 6,...]
    unnamed x7 -> x6, local copies, waits for them, and re-layouts: 4.18 us -> 2.12 us
    gather x4 -> x0, local copies, waits for them, and re-layouts: 1.14 us -> none  [body(): mix = mixing[zs][:, ys].reshape(1, NZ * NY * ROWS)]
where the time goes in v2:
time: 103 us; the launch traced here: 102 us
  Pallas kernels  99.3 us (96%)
  local copies, waits for them, and re-layouts  2.12 us (2%)
    pallas_call x1, Pallas kernels, body(): pl.pallas_call(kernel, out_shape=held, in_specs=[vmem] * 3 + [anym] * 6,...  96.9 us
    pallas_call x1, Pallas kernels, body(): pl.pallas_call(products, out_shape=(grad, grad, grad), in_specs=[vmem] *...  2.43 us
    unnamed x6, local copies, waits for them, and re-layouts  2.12 us

profile of v2, /device:TPU:1, one launch (start us, length us, event | category | flops | bytes accessed | tf_op | source)
XLA Modules:
  0.0 102.2 jit_solution(3708842385615217889)
XLA Ops:
  0.6 0.0 copy-start
  0.6 0.7 copy-done
  1.4 0.0 copy-start.1
  1.4 0.7 copy-done.1
  2.1 0.0 copy-start.2
  2.1 0.7 copy-done.2
  2.8 96.9 %distill.1 = (bf16[2,8,64,1024]{3,2,1,0:T(8,128)(2,1)S(1)}, bf16[2,8,64,1024]{3,2,1,0:T(8,128)(2,1)S(1)}, bf16[256,512]{1,0:T(8,128)(2,1)S(1)}, bf16[256,512]{1,0:T(8,128)(2,1)S(1)}, bf16[256,512]{1,0:T(8,128)(2,1)S(1)}) custom-call(bf16[8,2048]{1,0:T(8,128)(2,1)S(1)} %copy-done, s32[2,512]{1,0:T(2,128)S(1)} %bitcast.2, f32[2,512]{1,0:T(2,128)S(1)} %bitcast.3, ...), custom_call_target="tpu_custom_call" | custom-call | flops 6000000000 | bytes 12000000 | tf_op jit(solution)/shard_map/distill/pallas_call | solution.py:369
  99.6 2.4 %products.1 = (bf16[1,224,2048]{2,1,0:T(8,128)(2,1)}, bf16[1,224,2048]{2,1,0:T(8,128)(2,1)}, bf16[1,224,2048]{2,1,0:T(8,128)(2,1)}) custom-call(bf16[2,8,64,1024]{3,2,1,0:T(8,128)(2,1)S(1)} %get-tuple-element.8.tok, bf16[2,8,64,1024]{3,2,1,0:T(8,128)(2,1)S(1)} %get-tuple-element.9.res, bf16[256,512]{1,0:T(8,128)(2,1)S(1)} %get-tuple-element.10.pgrad, ...), custom_call_target="tpu_custom_call" | custom-call | flops 1500000000 | bytes 3000000 | tf_op jit(solution)/shard_map/products/pallas_call | solution.py:410
Async XLA Ops:
  0.6 0.8 copy-start
  1.4 0.7 copy-start.1
  2.1 0.7 copy-start.2

commit v3 on v2

v3 whole, which is shorter than its diff:
```python
import jax
import jax.numpy as jnp
from jax import lax
from jax.experimental import pallas as pl
from jax.experimental.pallas import tpu as pltpu
from jax.sharding import PartitionSpec as P

MESH = pl.DeviceIdType.MESH
F32, BF16 = jnp.float32, jnp.bfloat16
NX, NY, NZ = 4, 4, 8
ROWS = 16
WIDTH, HALF = 2048, 1024
TEACH, STUD = 448, 224
TQ, SQ = 112, 64
HQ = TQ + SQ
CHUNK, PARTS, SLABS = 128, 4, 2
TOKENS = CHUNK * PARTS
ORDER = (0, 1, 7, 2, 6, 3, 5, 4)
POS = tuple(ORDER.index(k) for k in range(NZ))
PC = 256
ZSEND = ((7,), (1, 6), (2, 5), (3, 4))
NSEM = 176
RELAY = (1, 1, 1, 1)
NT = (((1,), (1,)), ((), ()))


PROGRAM = (
    "X0 Q1A.0 Q1A.1 P1A ",
    "Q1A.2 Q1A.3 SA.0 LW ",
    "P2A.0 P2A.1 P2A.2 LD ",
    "MIX P2A.3 SA.1 SA.2 ",
    "KA.0 SA.3 O.0 KA.1 ",
    "B.0 O.1 KA.2 B.1 ",
    "R.0 KA.3 O.2 B.2 ",
    "O.3 B.3 R.1 R.2 ",
    "R.3 A.2 A.3 A.1 ",
    "E.2 A.0 E.3 F1.2 ",
    "E.1 F1.3 E.0 F1.1 ",
    "F1.0 F2.3 F2.2 F2.1 ",
    "F2.0 FP FQ Q1G.0 ",
    "Q1G.3 Q1G.1 FF P1G ",
    "SG.0 Q1G.2 P2G.3 FAC ",
    "P2G.0 P2G.1 SG.1 SG.3 ",
    "P2G.2 KG.0 SG.2 KG.1 ",
    "H.0 KG.3 H.1 KG.2 ",
    "HM H.3 HS.0 H.2 ",
    "HS.1 HS.3 HS.2 SL.3 ",
    "SL.1 SL.0 SL.2 ",
)


def dot(a, b, dims=(((1,), (0,)), ((), ()))):
    return lax.dot_general(a, b, dims, preferred_element_type=F32)


def kernel(
    tokens, routes, weights, tgate, tup, tdown, sgate, sup, sdown,
    tok, res, pgrad, lgrad, hm,
    tin, rin, win, w1, wd, tf, blk, mix, bacc, psend, prec, pass_on, hall, fac,
    fcore, rcore, facc, fsend, rz, ry, qsend, rqz, ysend, rpy,
    isend, irec, iown, hgrad, lsem, ssem, rsem,
):
    ix, iz, ie = lax.axis_index("dp"), lax.axis_index("neuron"), lax.axis_index("expert")
    iy, ic = ie // 2, lax.rem(ie, 2)
    oc = 1 - ic

    def dev(x=0, y=0, z=0, c=0):
        core = oc if c else ic
        return (lax.rem(ix + x, NX), lax.rem(iz + z, NZ), lax.rem(iy + y, NY) * 2 + core)

    partners = (
        [dev(x=k) for k in range(1, NX)] + [dev(y=k) for k in range(1, NY)]
        + [dev(z=k) for k in range(1, NZ)] + [dev(c=1)]
    )
    barrier = pltpu.get_barrier_semaphore()
    for p in partners:
        pl.semaphore_signal(barrier, inc=1, device_id=p, device_id_type=MESH)

    loads = []

    def load(src, dst):
        cp = pltpu.make_async_copy(src, dst, lsem.at[len(loads)])
        cp.start()
        loads.append(cp)

    load(tokens, tin)
    load(routes, rin)
    load(weights, win)
    zero = jnp.zeros((SQ // 2, HALF), BF16)
    for h in range(2):
        w1[h, 3, TQ + 32:HQ] = zero
        w1[h, 3, HQ + TQ + 32:] = zero
        wd[h, 3, TQ + 32:HQ] = zero
    for j in range(NX):
        n = SQ if j < 3 else SQ // 2
        for h in range(2):
            cols = pl.ds(h * HALF, HALF)
            load(tgate.at[pl.ds(j * TQ, TQ), cols], w1.at[h, j, pl.ds(0, TQ)])
            load(sgate.at[0, pl.ds(j * SQ, n), cols], w1.at[h, j, pl.ds(TQ, n)])
            load(tup.at[pl.ds(j * TQ, TQ), cols], w1.at[h, j, pl.ds(HQ, TQ)])
            load(sup.at[0, pl.ds(j * SQ, n), cols], w1.at[h, j, pl.ds(HQ + TQ, n)])
    n_w1 = len(loads)
    for j in range(NX):
        n = SQ if j < 3 else SQ // 2
        for h in range(2):
            cols = pl.ds(h * HALF, HALF)
            load(tdown.at[pl.ds(j * TQ, TQ), cols], wd.at[h, j, pl.ds(0, TQ)])
            load(sdown.at[0, pl.ds(j * SQ, n), cols], wd.at[h, j, pl.ds(TQ, n)])
    for cp in loads[:3]:
        cp.wait()

    for h in range(2):
        tf[h] = tin[:, h * HALF:(h + 1) * HALF].astype(F32)
    blk[pl.ds(pl.multiple_of(ic * 8, 8), 8), :] = tf[ic]
    pl.semaphore_wait(barrier, len(partners))

    sent = []

    def send(src, dst, to):
        i = len(sent)
        cp = pltpu.make_async_remote_copy(
            src_ref=src, dst_ref=dst, send_sem=ssem.at[i], recv_sem=rsem.at[i],
            device_id=to, device_id_type=MESH,
        )
        cp.start()
        sent.append(cp)
        return cp

    landed = set()

    def arrived(copies):
        for c in copies:
            if id(c) not in landed:
                landed.add(id(c))
                c.wait_recv()

    def exchange():
        cp = send(tf.at[oc], blk.at[pl.ds(pl.multiple_of(ic * 8, 8), 8), :], dev(c=1))
        cp.wait_recv()
        tok[ic, 0, 0:ROWS] = blk[...].astype(BF16)

    pcols, qcols = pl.ds(0, PC), pl.ds(PC, HALF - PC)

    def rows(k):
        return pl.ds((k % NY) * ROWS, ROWS)

    def group(part):
        return pl.ds(part * SLABS, SLABS)

    cps = {}

    def gather_tasks(buf, name):
        own = buf.at[ic, 0, pl.ds(0, ROWS)]

        def y_first():
            cps["P1" + name] = [send(own.at[:, pcols], buf.at[ic, 0, rows(-k), pcols], dev(y=k)) for k in (2, 1, 3)]

        def z_first(part):
            cps["Q1" + name, part] = [
                send(own.at[:, qcols], buf.at[ic, POS[-k % NZ], pl.ds(0, ROWS), qcols], dev(z=k)) for k in ZSEND[part]
            ]

        def y_then_z(part):
            arrived(cps.pop("P1" + name, []))
            cps["P2" + name, part] = [
                send(buf.at[ic, 0, :, pcols], buf.at[ic, POS[-k % NZ], :, pcols], dev(z=k)) for k in ZSEND[part]
            ]

        def z_then_y(part):
            arrived(cps["Q1" + name, part])
            g = group(part)
            cps["S" + name, part] = [
                send(buf.at[ic, g, pl.ds(0, ROWS), qcols], buf.at[ic, g, rows(-k), qcols], dev(y=k)) for k in (2, 1, 3)
            ]

        def to_core(part):
            arrived(cps["P2" + name, part])
            arrived(cps["S" + name, part])
            cps["K" + name, part] = [send(buf.at[ic, group(part)], buf.at[ic, group(part)], dev(c=1))]

        return {"P1": y_first, "Q1": z_first, "P2": y_then_z, "S": z_then_y, "K": to_core}

    def piece(buf, h, part):
        return buf[h, part * SLABS:(part + 1) * SLABS].reshape(CHUNK, HALF)

    def own_half(part):
        arrived(cps["P2A", part])
        arrived(cps["SA", part])
        for d in range(NX):
            bacc[part, d] = dot(w1[ic, lax.rem(ix + d, NX)], piece(tok, ic, part), NT)

    def hidden_parts(part):
        arrived(cps["KA", part])
        out = []
        for d in (2, 1, 3, 0):
            val = bacc[part, d] + dot(w1[oc, lax.rem(ix + d, NX)], piece(tok, oc, part), NT)
            if d == 0 or (RELAY[part] and d != 2):
                bacc[part, d] = val
                continue
            psend[part, d] = val.astype(BF16)
            if RELAY[part]:
                cps["R", part] = [
                    send(psend.at[part, d, pl.ds(0, HQ)], pass_on.at[part, 0], dev(x=1)),
                    send(psend.at[part, d, pl.ds(HQ, HQ)], pass_on.at[part, 1], dev(x=3)),
                ]
            else:
                out.append(send(psend.at[part, d], prec.at[part, NX - d], dev(x=d)))
        cps["B", part] = out

    def relay(part):
        arrived(cps["R", part])
        for n, d in enumerate((1, 3)):
            mid = slice(n * HQ, n * HQ + HQ)
            rest = slice(HQ - n * HQ, 2 * HQ - n * HQ)
            psend[part, d, mid] = (bacc[part, d, mid] + pass_on[part, n].astype(F32)).astype(BF16)
            psend[part, d, rest] = bacc[part, d, rest].astype(BF16)
            cps["B", part].append(send(psend.at[part, d], prec.at[part, NX - d], dev(x=d)))

    def activate(part):
        arrived(cps["B", part])
        total = bacc[part, 0]
        for d in (1, 3) if RELAY[part] else (1, 2, 3):
            total = total + prec[part, d].astype(F32)
        pre, lift = total[:HQ], total[HQ:]
        s = jax.nn.sigmoid(pre)
        act = pre * s
        hidden = act * lift
        weight = mix[part, 0:1]
        hall[part, ix, 0:TQ] = (-hidden[:TQ]).astype(BF16)
        hall[part, ix, TQ:HQ] = (hidden[TQ:] * weight).astype(BF16)
        mine = hall.at[part, ix]
        cps["A", part] = [send(mine, mine, dev(x=d)) for d in (2, 1, 3)]
        slope = s * (1.0 + pre * (1.0 - s))
        fac[ix, part, 0] = (weight * (lift * slope)[TQ:]).astype(BF16)
        fac[ix, part, 1] = (weight * act[TQ:]).astype(BF16)

    def factors():
        cps["FAC"] = [send(fac.at[ix], fac.at[ix], dev(x=k)) for k in (2, 1, 3)]

    def outputs(part):
        arrived(cps["A", part])
        hidden = hall[part].reshape(NX * HQ, CHUNK).T
        fcore[part] = dot(hidden, wd[oc].reshape(NX * HQ, HALF)).astype(BF16)
        cps["E", part] = [send(fcore.at[part], rcore.at[part], dev(c=1))]
        facc[part] = dot(hidden, wd[ic].reshape(NX * HQ, HALF))

    def scatter_first(part):
        arrived(cps["E", part])
        total = facc[part] + rcore[part].astype(F32)
        facc[part] = total
        fsend[part * SLABS:(part + 1) * SLABS] = total.astype(BF16).reshape(SLABS, 64, HALF)
        cps["F1", part] = [
            send(fsend.at[group(part), rows(k), qcols], ry.at[part, NY - k], dev(y=k)) for k in (2, 1, 3)
        ]
        cps["F1P", part] = [
            send(fsend.at[pos, :, pcols], rz.at[POS[-ORDER[pos] % NZ]], dev(z=ORDER[pos]))
            for pos in range(part * SLABS, (part + 1) * SLABS) if ORDER[pos]
        ]

    def scatter_second(part):
        arrived(cps["F1", part])
        total = facc[part].reshape(SLABS, 64, HALF)[:, :ROWS, PC:]
        for d in range(1, NY):
            total = total + ry[part, d].astype(F32)
        if part == 0:
            ysend[0:ROWS, PC:] = total[0]
        qsend[part * SLABS:(part + 1) * SLABS] = total.astype(BF16)
        cps["F2", part] = [
            send(qsend.at[pos], rqz.at[POS[-ORDER[pos] % NZ]], dev(z=ORDER[pos]))
            for pos in range(part * SLABS, (part + 1) * SLABS) if ORDER[pos]
        ]

    def scatter_y():
        total = facc[0, 0:64, :PC]
        for part in range(PARTS):
            arrived(cps["F1P", part])
        for pos in range(1, NZ):
            total = total + rz[pos].astype(F32)
        ysend[:, :PC] = total
        rpy[0] = total.astype(BF16)
        cps["FP"] = [send(rpy.at[0, rows(k)], rpy.at[NY - k, pl.ds(0, ROWS)], dev(y=k)) for k in (2, 1, 3)]

    def residual_q():
        for part in range(PARTS):
            arrived(cps["F2", part])
        total = ysend[0:ROWS, PC:]
        for pos in range(1, NZ):
            total = total + rqz[pos].astype(F32)
        res[ic, 0, 0:ROWS, PC:] = total.astype(BF16)

    def residual_p():
        arrived(cps["FP"])
        total = ysend[0:ROWS, :PC]
        for k in range(1, NY):
            total = total + rpy[k, 0:ROWS].astype(F32)
        res[ic, 0, 0:ROWS, :PC] = total.astype(BF16)

    def mixing():
        m = jnp.sum(jnp.where(rin[...] == ie, win[...], 0.0), axis=0, keepdims=True)
        m = jnp.broadcast_to(m, (8, TOKENS))
        m = pltpu.roll(m, lax.rem(NZ - iz, NZ) * 64, 1)
        lane = lax.broadcasted_iota(jnp.int32, (8, TOKENS), 1)
        near = pltpu.roll(m, lax.rem(TOKENS - iy * ROWS, TOKENS), 1)
        far = pltpu.roll(m, 64 - iy * ROWS, 1)
        m = jnp.where(lax.rem(lane, 64) < 64 - iy * ROWS, near, far)
        low = lax.broadcasted_iota(jnp.int32, (8, CHUNK), 1) < 64
        for part in range(PARTS):
            two = []
            for side in range(2):
                k = ORDER[part * 2 + side]
                t = m[:, (k // 2) * CHUNK:(k // 2 + 1) * CHUNK]
                two.append(t if k % 2 == side else pltpu.roll(t, 64, 1))
            mix[part] = jnp.where(low, two[0], two[1])

    def hidden_grads(part):
        arrived(cps["KG", part])
        out = []
        for d in (2, 1, 3, 0):
            j = lax.rem(ix + d, NX)
            val = dot(wd[0, j, TQ:], piece(res, 0, part), NT) + dot(wd[1, j, TQ:], piece(res, 1, part), NT)
            if d == 0:
                iown[part] = val
            else:
                isend[part, d] = val.astype(BF16)
                out.append(send(isend.at[part, d], irec.at[part, NX - d], dev(x=d)))
        cps["H", part] = out

    def hidden_sum(part):
        arrived(cps["H", part])
        total = iown[part]
        for d in range(1, NX):
            total = total + irec[part, d].astype(F32)
        hgrad[part, ix] = total.astype(BF16)
        mine = hgrad.at[part, ix]
        cps["HS", part] = [send(mine, mine, dev(x=d)) for d in (2, 1, 3)]

    def slopes(part):
        arrived(cps["HS", part])
        arrived(cps.pop("FAC", []))
        cols = pl.ds(part * CHUNK, CHUNK)
        for j in range(NX):
            grad = hgrad[part, j].astype(F32)
            units = pl.ds(j * SQ, SQ)
            pgrad[units, cols] = (grad * fac[j, part, 0].astype(F32)).astype(BF16)
            lgrad[units, cols] = (grad * fac[j, part, 1].astype(F32)).astype(BF16)

    def weighted_hidden():
        for part in range(PARTS):
            for j in range(NX):
                hm[j * SQ:(j + 1) * SQ, part * CHUNK:(part + 1) * CHUNK] = hall[part, j, TQ:HQ]

    def weights_ready(first, last):
        for cp in loads[first:last]:
            cp.wait()

    tasks = {
        "X0": exchange, "MIX": mixing, "HM": weighted_hidden, "FAC": factors,
        "LW": lambda: weights_ready(3, n_w1), "LD": lambda: weights_ready(n_w1, None),
        "O": own_half, "B": hidden_parts, "R": relay, "A": activate, "E": outputs, "F1": scatter_first,
        "F2": scatter_second, "FP": scatter_y, "FQ": residual_q, "FF": residual_p, "H": hidden_grads,
        "HS": hidden_sum, "SL": slopes,
    }
    for name, buf in (("A", tok), ("G", res)):
        tasks.update({key + name: task for key, task in gather_tasks(buf, name).items()})
    for step in ("".join(PROGRAM)).split():
        key, _, part = step.partition(".")
        tasks[key](*([int(part)] if part else []))
    for cp in sent:
        cp.wait_send()


def products(tok, res, pgrad, lgrad, hm, ggate, gup, gdown, stage, sem):
    copies = []
    for n, (left, right, out) in enumerate(((hm, res, gdown), (pgrad, tok, ggate), (lgrad, tok, gup))):
        for h in range(2):
            val = dot(left[:STUD], right[h].reshape(TOKENS, HALF))
            stage[n, h] = val.astype(BF16)
            cp = pltpu.make_async_copy(stage.at[n, h], out.at[0, :, pl.ds(h * HALF, HALF)], sem.at[n, h])
            cp.start()
            copies.append(cp)
    for cp in copies:
        cp.wait()


def body(tokens, tgate, tup, tdown, sgate, sup, sdown, routes, route_weight):
    vmem, anym = pl.BlockSpec(memory_space=pltpu.VMEM), pl.BlockSpec(memory_space=pl.ANY)
    V = pltpu.VMEM
    held = (
        V((2, NZ, 64, HALF), BF16),
        V((2, NZ, 64, HALF), BF16),
        V((NX * SQ, TOKENS), BF16),
        V((NX * SQ, TOKENS), BF16),
        V((NX * SQ, TOKENS), BF16),
    )
    args = (tokens, routes.T, route_weight.T, tgate, tup, tdown, sgate, sup, sdown)
    parts = pl.pallas_call(
        kernel,
        out_shape=held,
        in_specs=[anym] * 9,
        out_specs=(vmem,) * 5,
        scratch_shapes=[
            V((8, WIDTH), BF16),
            V((2, TOKENS), jnp.int32),
            V((2, TOKENS), F32),
            V((2, NX, 2 * HQ, HALF), BF16),
            V((2, NX, HQ, HALF), BF16),
            V((2, 8, HALF), F32),
            V((ROWS, HALF), F32),
            V((PARTS, 8, CHUNK), F32),
            V((PARTS, NX, 2 * HQ, CHUNK), F32),
            V((PARTS, NX, 2 * HQ, CHUNK), BF16),
            V((PARTS, NX, 2 * HQ, CHUNK), BF16),
            V((PARTS, 2, HQ, CHUNK), BF16),
            V((PARTS, NX, HQ, CHUNK), BF16),
            V((NX, PARTS, 2, SQ, CHUNK), BF16),
            V((PARTS, CHUNK, HALF), BF16),
            V((PARTS, CHUNK, HALF), BF16),
            V((PARTS, CHUNK, HALF), F32),
            V((NZ, 64, HALF), BF16),
            V((NZ, 64, PC), BF16),
            V((PARTS, NY, SLABS, ROWS, HALF - PC), BF16),
            V((NZ, ROWS, HALF - PC), BF16),
            V((NZ, ROWS, HALF - PC), BF16),
            V((64, HALF), F32),
            V((NY, 64, PC), BF16),
            V((PARTS, NX, SQ, CHUNK), BF16),
            V((PARTS, NX, SQ, CHUNK), BF16),
            V((PARTS, SQ, CHUNK), F32),
            V((PARTS, NX, SQ, CHUNK), BF16),
            pltpu.SemaphoreType.DMA((64,)),
            pltpu.SemaphoreType.DMA((NSEM,)),
            pltpu.SemaphoreType.DMA((NSEM,)),
        ],
        compiler_params=pltpu.CompilerParams(
            collective_id=0, has_side_effects=True, vmem_limit_bytes=40 * 2**20
        ),
        cost_estimate=pl.CostEstimate(flops=6 * 10**9, bytes_accessed=12 * 10**6, transcendentals=10**6),
        name="distill",
    )(*(pltpu.with_memory_space_constraint(a, pltpu.HBM) for a in args))
    grad = jax.ShapeDtypeStruct((1, STUD, WIDTH), BF16)
    return pl.pallas_call(
        products,
        out_shape=(grad, grad, grad),
        in_specs=[vmem] * 5,
        out_specs=(anym,) * 3,
        scratch_shapes=[V((3, 2, STUD, HALF), BF16), pltpu.SemaphoreType.DMA((3, 2))],
        compiler_params=pltpu.CompilerParams(vmem_limit_bytes=16 * 2**20),
        cost_estimate=pl.CostEstimate(flops=15 * 10**8, bytes_accessed=3 * 10**6, transcendentals=0),
        name="products",
    )(*parts)


def solution(mesh):
    split = P(("neuron", "expert"), "dp")
    expert = P("expert", "neuron", "dp")
    return jax.shard_map(
        body,
        mesh=mesh,
        in_specs=(split, split, split, split, expert, expert, expert, P(), P()),
        out_specs=(expert, expert, expert),
        check_vma=False,
    )
```

time: 103 us -> 88.7 us (0.86)
  Pallas kernels: 99.3 us -> 87.6 us
  local copies, waits for them, and re-layouts: 2.12 us -> 0 us
    pallas_call x1, Pallas kernels: 96.9 us -> 85.2 us  [body(): pl.pallas_call(kernel, out_shape=held, in_specs=[anym] * 9, out_specs=(vm...]
    unnamed x6 -> x0, local copies, waits for them, and re-layouts: 2.12 us -> none
where the time goes in v3:
time: 88.7 us; the launch traced here: 88.4 us
  Pallas kernels  87.6 us (99%)
    pallas_call x1, Pallas kernels, body(): pl.pallas_call(kernel, out_shape=held, in_specs=[anym] * 9, out_specs=(vm...  85.2 us
    pallas_call x1, Pallas kernels, body(): pl.pallas_call(products, out_shape=(grad, grad, grad), in_specs=[vmem] *...  2.43 us

profile of v3, /device:TPU:1, one launch (start us, length us, event | category | flops | bytes accessed | tf_op | source)
XLA Modules:
  0.0 88.4 jit_solution(2634047374982534174)
XLA Ops:
  0.6 85.2 %distill.1 = (bf16[2,8,64,1024]{3,2,1,0:T(8,128)(2,1)S(1)}, bf16[2,8,64,1024]{3,2,1,0:T(8,128)(2,1)S(1)}, bf16[256,512]{1,0:T(8,128)(2,1)S(1)}, bf16[256,512]{1,0:T(8,128)(2,1)S(1)}, bf16[256,512]{1,0:T(8,128)(2,1)S(1)}) custom-call(bf16[8,2048]{1,0:T(8,128)(2,1)} %tokens.1, s32[2,512]{1,0:T(2,128)} %bitcast.2, f32[2,512]{1,0:T(2,128)} %bitcast.3, ...), custom_call_target="tpu_custom_call" | custom-call | flops 6000000000 | bytes 12000000 | tf_op jit(solution)/shard_map/distill/pallas_call | solution.py:396
  85.9 2.4 %products.1 = (bf16[1,224,2048]{2,1,0:T(8,128)(2,1)}, bf16[1,224,2048]{2,1,0:T(8,128)(2,1)}, bf16[1,224,2048]{2,1,0:T(8,128)(2,1)}) custom-call(bf16[2,8,64,1024]{3,2,1,0:T(8,128)(2,1)S(1)} %get-tuple-element.8.tok, bf16[2,8,64,1024]{3,2,1,0:T(8,128)(2,1)S(1)} %get-tuple-element.9.res, bf16[256,512]{1,0:T(8,128)(2,1)S(1)} %get-tuple-element.10.pgrad, ...), custom_call_target="tpu_custom_call" | custom-call | flops 1500000000 | bytes 3000000 | tf_op jit(solution)/shard_map/products/pallas_call | solution.py:441

commit v4 on v3

--- a/solution.py
+++ b/solution.py
@@ -20,32 +20,34 @@
 PC = 256
 ZSEND = ((7,), (1, 6), (2, 5), (3, 4))
 NSEM = 176
+DRELAY = (0, 0, 0, 0)
+DIRECT = (0, 0, 0, 1)
 RELAY = (1, 1, 1, 1)
 NT = (((1,), (1,)), ((), ()))
 
 
 PROGRAM = (
-    "X0 Q1A.0 Q1A.1 P1A ",
-    "Q1A.2 Q1A.3 SA.0 LW ",
-    "P2A.0 P2A.1 P2A.2 LD ",
-    "MIX P2A.3 SA.1 SA.2 ",
-    "KA.0 SA.3 O.0 KA.1 ",
-    "B.0 O.1 KA.2 B.1 ",
-    "R.0 KA.3 O.2 B.2 ",
-    "O.3 B.3 R.1 R.2 ",
-    "R.3 A.2 A.3 A.1 ",
-    "E.2 A.0 E.3 F1.2 ",
-    "E.1 F1.3 E.0 F1.1 ",
-    "F1.0 F2.3 F2.2 F2.1 ",
-    "F2.0 FP FQ Q1G.0 ",
-    "Q1G.3 Q1G.1 FF P1G ",
-    "SG.0 Q1G.2 P2G.3 FAC ",
-    "P2G.0 P2G.1 SG.1 SG.3 ",
-    "P2G.2 KG.0 SG.2 KG.1 ",
-    "H.0 KG.3 H.1 KG.2 ",
-    "HM H.3 HS.0 H.2 ",
-    "HS.1 HS.3 HS.2 SL.3 ",
-    "SL.1 SL.0 SL.2 ",
+    "X0 Q1A.0 Q1A.1 Q1A.3 ",
+    "P1A LD1 Q1A.2 SA.0 ",
+    "P2A.0 P2A.1 P2A.3 P2A.2 ",
+    "LD2 SA.1 SA.3 KA.0 ",
+    "O.0 SA.2 KA.1 B.0 ",
+    "O.1 KA.3 B.1 R.0 ",
+    "KA.2 O.3 MIX B.3 ",
+    "O.2 B.2 A.0 R.3 ",
+    "R.2 R.1 A.3 E.0 ",
+    "A.2 A.1 F1.0 E.3 ",
+    "E.2 F1.3 E.1 F1.2 ",
+    "F2.0 F1.1 HM F2.3 ",
+    "F2.2 F2.1 FAC FP ",
+    "FQ Q1G.0 FF Q1G.1 ",
+    "P1G Q1G.2 Q1G.3 SG.0 ",
+    "P2G.0 P2G.1 P2G.3 SG.1 ",
+    "P2G.2 SG.2 KG.0 SG.3 ",
+    "KG.1 H.0 KG.2 H.1 ",
+    "KG.3 HS.0 H.2 H.3 ",
+    "HS.1 HS.2 GD SL.1 ",
+    "SL.3 SL.0 SL.2 ",
 )
 
 
@@ -55,10 +57,10 @@
 
 def kernel(
     tokens, routes, weights, tgate, tup, tdown, sgate, sup, sdown,
-    tok, res, pgrad, lgrad, hm,
-    tin, rin, win, w1, wd, tf, blk, mix, bacc, psend, prec, pass_on, hall, fac,
+    tok, gd, pgrad, lgrad,
+    res, hm, tin, rin, win, w1, wd, tf, blk, mix, bacc, psend, prec, pass_on, hall, fac,
     fcore, rcore, facc, fsend, rz, ry, qsend, rqz, ysend, rpy,
-    isend, irec, iown, hgrad, lsem, ssem, rsem,
+    isend, irec, iall, iown, hgrad, lsem, ssem, rsem,
 ):
     ix, iz, ie = lax.axis_index("dp"), lax.axis_index("neuron"), lax.axis_index("expert")
     iy, ic = ie // 2, lax.rem(ie, 2)
@@ -86,28 +88,42 @@
     load(tokens, tin)
     load(routes, rin)
     load(weights, win)
-    zero = jnp.zeros((SQ // 2, HALF), BF16)
-    for h in range(2):
-        w1[h, 3, TQ + 32:HQ] = zero
-        w1[h, 3, HQ + TQ + 32:] = zero
-        wd[h, 3, TQ + 32:HQ] = zero
-    for j in range(NX):
-        n = SQ if j < 3 else SQ // 2
+    n_w1, n_all = 3 + 8 * NX, 3 + 12 * NX
+
+    def load_first():
+        zero = jnp.zeros((SQ // 2, HALF), BF16)
         for h in range(2):
-            cols = pl.ds(h * HALF, HALF)
-            load(tgate.at[pl.ds(j * TQ, TQ), cols], w1.at[h, j, pl.ds(0, TQ)])
-            load(sgate.at[0, pl.ds(j * SQ, n), cols], w1.at[h, j, pl.ds(TQ, n)])
-            load(tup.at[pl.ds(j * TQ, TQ), cols], w1.at[h, j, pl.ds(HQ, TQ)])
-            load(sup.at[0, pl.ds(j * SQ, n), cols], w1.at[h, j, pl.ds(HQ + TQ, n)])
-    n_w1 = len(loads)
-    for j in range(NX):
-        n = SQ if j < 3 else SQ // 2
+            w1[h, 3, TQ + 32:HQ] = zero
+            w1[h, 3, HQ + TQ + 32:] = zero
+        for j in range(NX):
+            n = SQ if j < 3 else SQ // 2
+            for h in range(2):
+                cols = pl.ds(h * HALF, HALF)
+                load(tgate.at[pl.ds(j * TQ, TQ), cols], w1.at[h, j, pl.ds(0, TQ)])
+                load(sgate.at[0, pl.ds(j * SQ, n), cols], w1.at[h, j, pl.ds(TQ, n)])
+                load(tup.at[pl.ds(j * TQ, TQ), cols], w1.at[h, j, pl.ds(HQ, TQ)])
+                load(sup.at[0, pl.ds(j * SQ, n), cols], w1.at[h, j, pl.ds(HQ + TQ, n)])
+
+    def load_down():
+        zero = jnp.zeros((SQ // 2, HALF), BF16)
         for h in range(2):
-            cols = pl.ds(h * HALF, HALF)
-            load(tdown.at[pl.ds(j * TQ, TQ), cols], wd.at[h, j, pl.ds(0, TQ)])
-            load(sdown.at[0, pl.ds(j * SQ, n), cols], wd.at[h, j, pl.ds(TQ, n)])
-    for cp in loads[:3]:
-        cp.wait()
+            wd[h, 3, TQ + 32:HQ] = zero
+        for j in range(NX):
+            n = SQ if j < 3 else SQ // 2
+            for h in range(2):
+                cols = pl.ds(h * HALF, HALF)
+                load(tdown.at[pl.ds(j * TQ, TQ), cols], wd.at[h, j, pl.ds(0, TQ)])
+                load(sdown.at[0, pl.ds(j * SQ, n), cols], wd.at[h, j, pl.ds(TQ, n)])
+
+    loaded = set()
+
+    def weights_ready(first, last):
+        for i in range(first, last):
+            if i not in loaded:
+                loaded.add(i)
+                loads[i].wait()
+
+    weights_ready(0, 3)
 
     for h in range(2):
         tf[h] = tin[:, h * HALF:(h + 1) * HALF].astype(F32)
@@ -184,6 +200,7 @@
         return buf[h, part * SLABS:(part + 1) * SLABS].reshape(CHUNK, HALF)
 
     def own_half(part):
+        weights_ready(3, n_w1)
         arrived(cps["P2A", part])
         arrived(cps["SA", part])
         for d in range(NX):
@@ -229,7 +246,7 @@
         hall[part, ix, 0:TQ] = (-hidden[:TQ]).astype(BF16)
         hall[part, ix, TQ:HQ] = (hidden[TQ:] * weight).astype(BF16)
         mine = hall.at[part, ix]
-        cps["A", part] = [send(mine, mine, dev(x=d)) for d in (2, 1, 3)]
+        cps["A", part] = [send(mine, mine, dev(x=d)) for d in ((1, 3) if DRELAY[part] else (2, 1, 3))]
         slope = s * (1.0 + pre * (1.0 - s))
         fac[ix, part, 0] = (weight * (lift * slope)[TQ:]).astype(BF16)
         fac[ix, part, 1] = (weight * act[TQ:]).astype(BF16)
@@ -237,8 +254,17 @@
     def factors():
         cps["FAC"] = [send(fac.at[ix], fac.at[ix], dev(x=k)) for k in (2, 1, 3)]
 
+    def pass_hidden(part):
+        arrived(cps["A", part])
+        cps["DR", part] = []
+        for d, first, n in ((1, 0, 96), (3, 96, HQ - 96)):
+            piece_of = hall.at[part, lax.rem(ix + NX - d, NX), pl.ds(first, n)]
+            cps["DR", part].append(send(piece_of, piece_of, dev(x=d)))
+
     def outputs(part):
+        weights_ready(n_w1, n_all)
         arrived(cps["A", part])
+        arrived(cps.get(("DR", part), []))
         hidden = hall[part].reshape(NX * HQ, CHUNK).T
         fcore[part] = dot(hidden, wd[oc].reshape(NX * HQ, HALF)).astype(BF16)
         cps["E", part] = [send(fcore.at[part], rcore.at[part], dev(c=1))]
@@ -314,20 +340,21 @@
 
     def hidden_grads(part):
         arrived(cps["KG", part])
-        out = []
-        for d in (2, 1, 3, 0):
-            j = lax.rem(ix + d, NX)
-            val = dot(wd[0, j, TQ:], piece(res, 0, part), NT) + dot(wd[1, j, TQ:], piece(res, 1, part), NT)
-            if d == 0:
-                iown[part] = val
-            else:
-                isend[part, d] = val.astype(BF16)
-                out.append(send(isend.at[part, d], irec.at[part, NX - d], dev(x=d)))
+        left = [wd[h, :, TQ:].reshape(NX * SQ, HALF) for h in range(2)]
+        val = dot(left[0], piece(res, 0, part), NT) + dot(left[1], piece(res, 1, part), NT)
+        iown[part] = val.reshape(NX, SQ, CHUNK)
+        isend[part] = val.astype(BF16).reshape(NX, SQ, CHUNK)
+        if DIRECT[part]:
+            out = [send(isend.at[part], iall.at[part, NX - d], dev(x=d)) for d in (2, 1, 3)]
+        else:
+            out = [
+                send(isend.at[part, lax.rem(ix + d, NX)], irec.at[part, NX - d], dev(x=d)) for d in (2, 1, 3)
+            ]
         cps["H", part] = out
 
     def hidden_sum(part):
         arrived(cps["H", part])
-        total = iown[part]
+        total = iown[part, ix]
         for d in range(1, NX):
             total = total + irec[part, d].astype(F32)
         hgrad[part, ix] = total.astype(BF16)
@@ -335,9 +362,16 @@
         cps["HS", part] = [send(mine, mine, dev(x=d)) for d in (2, 1, 3)]
 
     def slopes(part):
-        arrived(cps["HS", part])
-        arrived(cps.pop("FAC", []))
+        arrived(cps["H" if DIRECT[part] else "HS", part])
+        arrived(cps["FAC"])
         cols = pl.ds(part * CHUNK, CHUNK)
+        if DIRECT[part]:
+            grad = iown[part].reshape(NX * SQ, CHUNK)
+            for d in range(1, NX):
+                grad = grad + iall[part, d].reshape(NX * SQ, CHUNK).astype(F32)
+            pgrad[:, cols] = (grad * fac[:, part, 0].reshape(NX * SQ, CHUNK).astype(F32)).astype(BF16)
+            lgrad[:, cols] = (grad * fac[:, part, 1].reshape(NX * SQ, CHUNK).astype(F32)).astype(BF16)
+            return
         for j in range(NX):
             grad = hgrad[part, j].astype(F32)
             units = pl.ds(j * SQ, SQ)
@@ -349,13 +383,13 @@
             for j in range(NX):
                 hm[j * SQ:(j + 1) * SQ, part * CHUNK:(part + 1) * CHUNK] = hall[part, j, TQ:HQ]
 
-    def weights_ready(first, last):
-        for cp in loads[first:last]:
-            cp.wait()
+    def down_product():
+        for h in range(2):
+            gd[h] = dot(hm[:STUD], res[h].reshape(TOKENS, HALF)).astype(BF16)
 
     tasks = {
         "X0": exchange, "MIX": mixing, "HM": weighted_hidden, "FAC": factors,
-        "LW": lambda: weights_ready(3, n_w1), "LD": lambda: weights_ready(n_w1, None),
+        "LD1": load_first, "LD2": load_down, "DR": pass_hidden, "GD": down_product,
         "O": own_half, "B": hidden_parts, "R": relay, "A": activate, "E": outputs, "F1": scatter_first,
         "F2": scatter_second, "FP": scatter_y, "FQ": residual_q, "FF": residual_p, "H": hidden_grads,
         "HS": hidden_sum, "SL": slopes,
@@ -369,15 +403,20 @@
         cp.wait_send()
 
 
-def products(tok, res, pgrad, lgrad, hm, ggate, gup, gdown, stage, sem):
+def products(tok, gd, pgrad, lgrad, ggate, gup, gdown, stage, sem):
     copies = []
-    for n, (left, right, out) in enumerate(((hm, res, gdown), (pgrad, tok, ggate), (lgrad, tok, gup))):
+
+    def write(src, out, n, h):
+        cp = pltpu.make_async_copy(src, out.at[0, :, pl.ds(h * HALF, HALF)], sem.at[n, h])
+        cp.start()
+        copies.append(cp)
+
+    for h in range(2):
+        write(gd.at[h], gdown, 2, h)
+    for n, (left, out) in enumerate(((pgrad, ggate), (lgrad, gup))):
         for h in range(2):
-            val = dot(left[:STUD], right[h].reshape(TOKENS, HALF))
-            stage[n, h] = val.astype(BF16)
-            cp = pltpu.make_async_copy(stage.at[n, h], out.at[0, :, pl.ds(h * HALF, HALF)], sem.at[n, h])
-            cp.start()
-            copies.append(cp)
+            stage[n, h] = dot(left[:STUD], tok[h].reshape(TOKENS, HALF)).astype(BF16)
+            write(stage.at[n, h], out, n, h)
     for cp in copies:
         cp.wait()
 
@@ -387,8 +426,7 @@
     V = pltpu.VMEM
     held = (
         V((2, NZ, 64, HALF), BF16),
-        V((2, NZ, 64, HALF), BF16),
-        V((NX * SQ, TOKENS), BF16),
+        V((2, STUD, HALF), BF16),
         V((NX * SQ, TOKENS), BF16),
         V((NX * SQ, TOKENS), BF16),
     )
@@ -397,8 +435,10 @@
         kernel,
         out_shape=held,
         in_specs=[anym] * 9,
-        out_specs=(vmem,) * 5,
+        out_specs=(vmem,) * 4,
         scratch_shapes=[
+            V((2, NZ, 64, HALF), BF16),
+            V((NX * SQ, TOKENS), BF16),
             V((8, WIDTH), BF16),
             V((2, TOKENS), jnp.int32),
             V((2, TOKENS), F32),
@@ -425,7 +465,8 @@
             V((NY, 64, PC), BF16),
             V((PARTS, NX, SQ, CHUNK), BF16),
             V((PARTS, NX, SQ, CHUNK), BF16),
-            V((PARTS, SQ, CHUNK), F32),
+            V((PARTS, NX, NX, SQ, CHUNK), BF16),
+            V((PARTS, NX, SQ, CHUNK), F32),
             V((PARTS, NX, SQ, CHUNK), BF16),
             pltpu.SemaphoreType.DMA((64,)),
             pltpu.SemaphoreType.DMA((NSEM,)),
@@ -441,9 +482,9 @@
     return pl.pallas_call(
         products,
         out_shape=(grad, grad, grad),
-        in_specs=[vmem] * 5,
+        in_specs=[vmem] * 4,
         out_specs=(anym,) * 3,
-        scratch_shapes=[V((3, 2, STUD, HALF), BF16), pltpu.SemaphoreType.DMA((3, 2))],
+        scratch_shapes=[V((2, 2, STUD, HALF), BF16), pltpu.SemaphoreType.DMA((3, 2))],
         compiler_params=pltpu.CompilerParams(vmem_limit_bytes=16 * 2**20),
         cost_estimate=pl.CostEstimate(flops=15 * 10**8, bytes_accessed=3 * 10**6, transcendentals=0),
         name="products",

time: 88.7 us -> 88.2 us (level)
  no operation moved by 1% of the time
where the time goes in v4:
time: 88.2 us; the launch traced here: 88 us
  Pallas kernels  87.2 us (99%)
    pallas_call x1, Pallas kernels, body(): pl.pallas_call(kernel, out_shape=held, in_specs=[anym] * 9, out_specs=(vm...  85.3 us
    pallas_call x1, Pallas kernels, body(): pl.pallas_call(products, out_shape=(grad, grad, grad), in_specs=[vmem] *...  1.95 us

profile of v4, /device:TPU:1, one launch (start us, length us, event | category | flops | bytes accessed | tf_op | source)
XLA Modules:
  0.0 88.0 jit_solution(11590590689070146493)
XLA Ops:
  0.6 85.3 %distill.1 = (bf16[2,8,64,1024]{3,2,1,0:T(8,128)(2,1)S(1)}, bf16[2,224,1024]{2,1,0:T(8,128)(2,1)S(1)}, bf16[256,512]{1,0:T(8,128)(2,1)S(1)}, bf16[256,512]{1,0:T(8,128)(2,1)S(1)}) custom-call(bf16[8,2048]{1,0:T(8,128)(2,1)} %tokens.1, s32[2,512]{1,0:T(2,128)} %bitcast.2, f32[2,512]{1,0:T(2,128)} %bitcast.3, bf16[448,2048]{1,0:T(8,128)(2,1)} %tgate.1, ...), custom_call_target="tpu_custom_call" | custom-call | flops 6000000000 | bytes 12000000 | tf_op jit(solution)/shard_map/distill/pallas_call | solution.py:434
  85.9 2.0 %products.1 = (bf16[1,224,2048]{2,1,0:T(8,128)(2,1)}, bf16[1,224,2048]{2,1,0:T(8,128)(2,1)}, bf16[1,224,2048]{2,1,0:T(8,128)(2,1)}) custom-call(bf16[2,8,64,1024]{3,2,1,0:T(8,128)(2,1)S(1)} %get-tuple-element.7.tok, bf16[2,224,1024]{2,1,0:T(8,128)(2,1)S(1)} %get-tuple-element.8.gd, bf16[256,512]{1,0:T(8,128)(2,1)S(1)} %get-tuple-element.9.pgrad, ...), custom_call_target="tpu_custom_call" | custom-call | flops 1500000000 | bytes 3000000 | tf_op jit(solution)/shard_map/products/pallas_call | solution.py:482

commit v5 on v4

--- a/solution.py
+++ b/solution.py
@@ -19,35 +19,35 @@
 POS = tuple(ORDER.index(k) for k in range(NZ))
 PC = 256
 ZSEND = ((7,), (1, 6), (2, 5), (3, 4))
-NSEM = 176
+NSEM = 192
 DRELAY = (0, 0, 0, 0)
-DIRECT = (0, 0, 0, 1)
+DIRECT = (0, 1, 1, 0)
 RELAY = (1, 1, 1, 1)
 NT = (((1,), (1,)), ((), ()))
 
 
 PROGRAM = (
-    "X0 Q1A.0 Q1A.1 Q1A.3 ",
-    "P1A LD1 Q1A.2 SA.0 ",
-    "P2A.0 P2A.1 P2A.3 P2A.2 ",
-    "LD2 SA.1 SA.3 KA.0 ",
-    "O.0 SA.2 KA.1 B.0 ",
-    "O.1 KA.3 B.1 R.0 ",
-    "KA.2 O.3 MIX B.3 ",
-    "O.2 B.2 A.0 R.3 ",
-    "R.2 R.1 A.3 E.0 ",
-    "A.2 A.1 F1.0 E.3 ",
-    "E.2 F1.3 E.1 F1.2 ",
-    "F2.0 F1.1 HM F2.3 ",
-    "F2.2 F2.1 FAC FP ",
-    "FQ Q1G.0 FF Q1G.1 ",
-    "P1G Q1G.2 Q1G.3 SG.0 ",
-    "P2G.0 P2G.1 P2G.3 SG.1 ",
-    "P2G.2 SG.2 KG.0 SG.3 ",
-    "KG.1 H.0 KG.2 H.1 ",
-    "KG.3 HS.0 H.2 H.3 ",
-    "HS.1 HS.2 GD SL.1 ",
-    "SL.3 SL.0 SL.2 ",
+    "X0 Q1A.0 Q1A.2 Q1A.3 ",
+    "P1A LD1 MIX Q1A.1 ",
+    "SA.0 P2A.0 P2A.2 P2A.3 ",
+    "LD2 SA.2 KA.0 SA.3 ",
+    "P2A.1 O.0 SA.1 B.0 ",
+    "KA.2 O.2 B.2 KA.3 ",
+    "R.0 O.3 KA.1 O.1 ",
+    "B.3 B.1 R.2 R.3 ",
+    "R.1 A.2 A.3 A.1 ",
+    "A.0 E.2 E.3 F1.2 ",
+    "E.1 F1.3 E.0 FAC ",
+    "F1.1 F1.0 F2.3 F2.2 ",
+    "F2.1 F2.0 FP FQ ",
+    "Q1G.0 Q1G.1 FF Q1G.3 ",
+    "P1G Q1G.2 SG.0 P2G.1 ",
+    "P2G.0 P2G.3 SG.1 P2G.2 ",
+    "SG.3 KG.0 SG.2 KG.1 ",
+    "H.0 HM H.1 KG.3 ",
+    "KG.2 H.3 HS.0 H.2 ",
+    "HS.3 SL.0 GD SL.2 ",
+    "SL.1 SL.3 ",
 )
 
 
@@ -169,7 +169,10 @@
         own = buf.at[ic, 0, pl.ds(0, ROWS)]
 
         def y_first():
-            cps["P1" + name] = [send(own.at[:, pcols], buf.at[ic, 0, rows(-k), pcols], dev(y=k)) for k in (2, 1, 3)]
+            for key, cols in (("P1", pcols), ("PQ", qcols)):
+                cps[key + name] = [
+                    send(own.at[:, cols], buf.at[ic, 0, rows(-k), cols], dev(y=k)) for k in (2, 1, 3)
+                ]
 
         def z_first(part):
             cps["Q1" + name, part] = [
@@ -184,7 +187,7 @@
 
         def z_then_y(part):
             arrived(cps["Q1" + name, part])
-            g = group(part)
+            g = group(part) if part else pl.ds(1, SLABS - 1)
             cps["S" + name, part] = [
                 send(buf.at[ic, g, pl.ds(0, ROWS), qcols], buf.at[ic, g, rows(-k), qcols], dev(y=k)) for k in (2, 1, 3)
             ]
@@ -192,6 +195,8 @@
         def to_core(part):
             arrived(cps["P2" + name, part])
             arrived(cps["S" + name, part])
+            if part == 0:
+                arrived(cps["PQ" + name])
             cps["K" + name, part] = [send(buf.at[ic, group(part)], buf.at[ic, group(part)], dev(c=1))]
 
         return {"P1": y_first, "Q1": z_first, "P2": y_then_z, "S": z_then_y, "K": to_core}
@@ -203,6 +208,8 @@
         weights_ready(3, n_w1)
         arrived(cps["P2A", part])
         arrived(cps["SA", part])
+        if part == 0:
+            arrived(cps["PQA"])
         for d in range(NX):
             bacc[part, d] = dot(w1[ic, lax.rem(ix + d, NX)], piece(tok, ic, part), NT)
 

time: 88.2 us -> 87.1 us (0.988)
  Pallas kernels: 87.2 us -> 86.2 us
    pallas_call x1, Pallas kernels: 85.3 us -> 84.2 us  [body(): pl.pallas_call(kernel, out_shape=held, in_specs=[anym] * 9, out_specs=(vm...]
where the time goes in v5:
time: 87.1 us; the launch traced here: 87 us
  Pallas kernels  86.2 us (99%)
    pallas_call x1, Pallas kernels, body(): pl.pallas_call(kernel, out_shape=held, in_specs=[anym] * 9, out_specs=(vm...  84.2 us
    pallas_call x1, Pallas kernels, body(): pl.pallas_call(products, out_shape=(grad, grad, grad), in_specs=[vmem] *...  1.95 us

profile of v5, /device:TPU:1, one launch (start us, length us, event | category | flops | bytes accessed | tf_op | source)
XLA Modules:
  0.0 87.0 jit_solution(13703101817218053054)
XLA Ops:
  0.6 84.2 %distill.1 = (bf16[2,8,64,1024]{3,2,1,0:T(8,128)(2,1)S(1)}, bf16[2,224,1024]{2,1,0:T(8,128)(2,1)S(1)}, bf16[256,512]{1,0:T(8,128)(2,1)S(1)}, bf16[256,512]{1,0:T(8,128)(2,1)S(1)}) custom-call(bf16[8,2048]{1,0:T(8,128)(2,1)} %tokens.1, s32[2,512]{1,0:T(2,128)} %bitcast.2, f32[2,512]{1,0:T(2,128)} %bitcast.3, bf16[448,2048]{1,0:T(8,128)(2,1)} %tgate.1, ...), custom_call_target="tpu_custom_call" | custom-call | flops 6000000000 | bytes 12000000 | tf_op jit(solution)/shard_map/distill/pallas_call | solution.py:441
  84.9 1.9 %products.1 = (bf16[1,224,2048]{2,1,0:T(8,128)(2,1)}, bf16[1,224,2048]{2,1,0:T(8,128)(2,1)}, bf16[1,224,2048]{2,1,0:T(8,128)(2,1)}) custom-call(bf16[2,8,64,1024]{3,2,1,0:T(8,128)(2,1)S(1)} %get-tuple-element.7.tok, bf16[2,224,1024]{2,1,0:T(8,128)(2,1)S(1)} %get-tuple-element.8.gd, bf16[256,512]{1,0:T(8,128)(2,1)S(1)} %get-tuple-element.9.pgrad, ...), custom_call_target="tpu_custom_call" | custom-call | flops 1500000000 | bytes 3000000 | tf_op jit(solution)/shard_map/products/pallas_call | solution.py:489

commit v6 on v5

--- a/solution.py
+++ b/solution.py
@@ -21,33 +21,35 @@
 ZSEND = ((7,), (1, 6), (2, 5), (3, 4))
 NSEM = 192
 DRELAY = (0, 0, 0, 0)
-DIRECT = (0, 1, 1, 0)
+DIRECT = (0, 0, 1, 1)
 RELAY = (1, 1, 1, 1)
 NT = (((1,), (1,)), ((), ()))
 
 
 PROGRAM = (
-    "X0 Q1A.0 Q1A.2 Q1A.3 ",
-    "P1A LD1 MIX Q1A.1 ",
+    "X0 Q1A.0 Q1A.2 P1A ",
+    "Q1A.3 MIX Q1A.1 LD1 ",
     "SA.0 P2A.0 P2A.2 P2A.3 ",
-    "LD2 SA.2 KA.0 SA.3 ",
-    "P2A.1 O.0 SA.1 B.0 ",
-    "KA.2 O.2 B.2 KA.3 ",
-    "R.0 O.3 KA.1 O.1 ",
-    "B.3 B.1 R.2 R.3 ",
-    "R.1 A.2 A.3 A.1 ",
-    "A.0 E.2 E.3 F1.2 ",
-    "E.1 F1.3 E.0 FAC ",
-    "F1.1 F1.0 F2.3 F2.2 ",
-    "F2.1 F2.0 FP FQ ",
-    "Q1G.0 Q1G.1 FF Q1G.3 ",
-    "P1G Q1G.2 SG.0 P2G.1 ",
-    "P2G.0 P2G.3 SG.1 P2G.2 ",
-    "SG.3 KG.0 SG.2 KG.1 ",
-    "H.0 HM H.1 KG.3 ",
-    "KG.2 H.3 HS.0 H.2 ",
-    "HS.3 SL.0 GD SL.2 ",
-    "SL.1 SL.3 ",
+    "SA.2 KA.0 SA.3 P2A.1 ",
+    "SA.1 O.0 B.0 KA.2 ",
+    "O.2 B.2 KA.3 R.0 ",
+    "KA.1 O.3 B.3 R.2 ",
+    "O.1 B.1 LD2 R.3 ",
+    "A.2 R.1 A.3 E.2 ",
+    "A.1 A.0 E.3 F1.2 ",
+    "F1.3 E.1 E.0 F1.1 ",
+    "F1.0 F2.3 F2.2 F2.1 ",
+    "FP FAC F2.0 WS ",
+    "FQ Q1G.0 FF P1G ",
+    "Q1G.1 Q1G.2 Q1G.3 WS ",
+    "SG.0 P2G.0 P2G.1 SG.1 ",
+    "P2G.2 P2G.3 SG.2 KG.0 ",
+    "HO.0 H.0 SG.3 KG.1 ",
+    "HO.1 KG.2 HO.2 H.1 ",
+    "HS.0 H.2 KG.3 HO.3 ",
+    "HS.1 H.3 HM WS ",
+    "SL.1 SL.0 GD SL.2 ",
+    "SL.3 ",
 )
 
 
@@ -143,6 +145,14 @@
         return cp
 
     landed = set()
+
+    left_off = [0]
+
+    def finish(spare):
+        last = max(len(sent) - spare, left_off[0])
+        for cp in sent[left_off[0]:last]:
+            cp.wait_send()
+        left_off[0] = last
 
     def arrived(copies):
         for c in copies:
@@ -345,10 +355,14 @@
                 two.append(t if k % 2 == side else pltpu.roll(t, 64, 1))
             mix[part] = jnp.where(low, two[0], two[1])
 
+    def own_hidden_grads(part):
+        left = wd[ic, :, TQ:].reshape(NX * SQ, HALF)
+        iown[part] = dot(left, piece(res, ic, part), NT).reshape(NX, SQ, CHUNK)
+
     def hidden_grads(part):
         arrived(cps["KG", part])
-        left = [wd[h, :, TQ:].reshape(NX * SQ, HALF) for h in range(2)]
-        val = dot(left[0], piece(res, 0, part), NT) + dot(left[1], piece(res, 1, part), NT)
+        left = wd[oc, :, TQ:].reshape(NX * SQ, HALF)
+        val = iown[part].reshape(NX * SQ, CHUNK) + dot(left, piece(res, oc, part), NT)
         iown[part] = val.reshape(NX, SQ, CHUNK)
         isend[part] = val.astype(BF16).reshape(NX, SQ, CHUNK)
         if DIRECT[part]:
@@ -396,9 +410,9 @@
 
     tasks = {
         "X0": exchange, "MIX": mixing, "HM": weighted_hidden, "FAC": factors,
-        "LD1": load_first, "LD2": load_down, "DR": pass_hidden, "GD": down_product,
+        "WS": lambda: finish(12), "LD1": load_first, "LD2": load_down, "DR": pass_hidden, "GD": down_product,
         "O": own_half, "B": hidden_parts, "R": relay, "A": activate, "E": outputs, "F1": scatter_first,
-        "F2": scatter_second, "FP": scatter_y, "FQ": residual_q, "FF": residual_p, "H": hidden_grads,
+        "F2": scatter_second, "FP": scatter_y, "FQ": residual_q, "FF": residual_p, "HO": own_hidden_grads, "H": hidden_grads,
         "HS": hidden_sum, "SL": slopes,
     }
     for name, buf in (("A", tok), ("G", res)):
@@ -406,8 +420,7 @@
     for step in ("".join(PROGRAM)).split():
         key, _, part = step.partition(".")
         tasks[key](*([int(part)] if part else []))
-    for cp in sent:
-        cp.wait_send()
+    finish(0)
 
 
 def products(tok, gd, pgrad, lgrad, ggate, gup, gdown, stage, sem):

time: 87.1 us -> 86.2 us (0.990)
  Pallas kernels: 86.2 us -> 85.3 us
    pallas_call x1, Pallas kernels: 84.2 us -> 83.3 us  [body(): pl.pallas_call(kernel, out_shape=held, in_specs=[anym] * 9, out_specs=(vm...]
where the time goes in v6:
time: 86.2 us; the launch traced here: 86.1 us
  Pallas kernels  85.3 us (99%)
    pallas_call x1, Pallas kernels, body(): pl.pallas_call(kernel, out_shape=held, in_specs=[anym] * 9, out_specs=(vm...  83.3 us
    pallas_call x1, Pallas kernels, body(): pl.pallas_call(products, out_shape=(grad, grad, grad), in_specs=[vmem] *...  1.95 us

profile of v6, /device:TPU:1, one launch (start us, length us, event | category | flops | bytes accessed | tf_op | source)
XLA Modules:
  0.0 86.1 jit_solution(3870619887251871665)
XLA Ops:
  0.6 83.3 %distill.1 = (bf16[2,8,64,1024]{3,2,1,0:T(8,128)(2,1)S(1)}, bf16[2,224,1024]{2,1,0:T(8,128)(2,1)S(1)}, bf16[256,512]{1,0:T(8,128)(2,1)S(1)}, bf16[256,512]{1,0:T(8,128)(2,1)S(1)}) custom-call(bf16[8,2048]{1,0:T(8,128)(2,1)} %tokens.1, s32[2,512]{1,0:T(2,128)} %bitcast.2, f32[2,512]{1,0:T(2,128)} %bitcast.3, bf16[448,2048]{1,0:T(8,128)(2,1)} %tgate.1, ...), custom_call_target="tpu_custom_call" | custom-call | flops 6000000000 | bytes 12000000 | tf_op jit(solution)/shard_map/distill/pallas_call | solution.py:454
  84.0 2.0 %products.1 = (bf16[1,224,2048]{2,1,0:T(8,128)(2,1)}, bf16[1,224,2048]{2,1,0:T(8,128)(2,1)}, bf16[1,224,2048]{2,1,0:T(8,128)(2,1)}) custom-call(bf16[2,8,64,1024]{3,2,1,0:T(8,128)(2,1)S(1)} %get-tuple-element.7.tok, bf16[2,224,1024]{2,1,0:T(8,128)(2,1)S(1)} %get-tuple-element.8.gd, bf16[256,512]{1,0:T(8,128)(2,1)S(1)} %get-tuple-element.9.pgrad, ...), custom_call_target="tpu_custom_call" | custom-call | flops 1500000000 | bytes 3000000 | tf_op jit(solution)/shard_map/products/pallas_call | solution.py:502

commit v7 on v6

--- a/solution.py
+++ b/solution.py
@@ -28,13 +28,13 @@
 
 PROGRAM = (
     "X0 Q1A.0 Q1A.2 P1A ",
-    "Q1A.3 MIX Q1A.1 LD1 ",
-    "SA.0 P2A.0 P2A.2 P2A.3 ",
+    "Q1A.3 Q1A.1 LD1 SA.0 ",
+    "P2A.0 P2A.2 P2A.3 LD2 ",
     "SA.2 KA.0 SA.3 P2A.1 ",
     "SA.1 O.0 B.0 KA.2 ",
     "O.2 B.2 KA.3 R.0 ",
     "KA.1 O.3 B.3 R.2 ",
-    "O.1 B.1 LD2 R.3 ",
+    "O.1 B.1 R.3 MIX ",
     "A.2 R.1 A.3 E.2 ",
     "A.1 A.0 E.3 F1.2 ",
     "F1.3 E.1 E.0 F1.1 ",

time: 86.2 us -> 86.4 us (level)
  no operation moved by 1% of the time
where the time goes in v7:
time: 86.4 us; the launch traced here: 86.3 us
  Pallas kernels  85.5 us (99%)
    pallas_call x1, Pallas kernels, body(): pl.pallas_call(kernel, out_shape=held, in_specs=[anym] * 9, out_specs=(vm...  83.5 us
    pallas_call x1, Pallas kernels, body(): pl.pallas_call(products, out_shape=(grad, grad, grad), in_specs=[vmem] *...  1.95 us

profile of v7, /device:TPU:1, one launch (start us, length us, event | category | flops | bytes accessed | tf_op | source)
XLA Modules:
  0.0 86.3 jit_solution(3052233665916554145)
XLA Ops:
  0.6 83.5 %distill.1 = (bf16[2,8,64,1024]{3,2,1,0:T(8,128)(2,1)S(1)}, bf16[2,224,1024]{2,1,0:T(8,128)(2,1)S(1)}, bf16[256,512]{1,0:T(8,128)(2,1)S(1)}, bf16[256,512]{1,0:T(8,128)(2,1)S(1)}) custom-call(bf16[8,2048]{1,0:T(8,128)(2,1)} %tokens.1, s32[2,512]{1,0:T(2,128)} %bitcast.2, f32[2,512]{1,0:T(2,128)} %bitcast.3, bf16[448,2048]{1,0:T(8,128)(2,1)} %tgate.1, ...), custom_call_target="tpu_custom_call" | custom-call | flops 6000000000 | bytes 12000000 | tf_op jit(solution)/shard_map/distill/pallas_call | solution.py:454
  84.2 1.9 %products.1 = (bf16[1,224,2048]{2,1,0:T(8,128)(2,1)}, bf16[1,224,2048]{2,1,0:T(8,128)(2,1)}, bf16[1,224,2048]{2,1,0:T(8,128)(2,1)}) custom-call(bf16[2,8,64,1024]{3,2,1,0:T(8,128)(2,1)S(1)} %get-tuple-element.7.tok, bf16[2,224,1024]{2,1,0:T(8,128)(2,1)S(1)} %get-tuple-element.8.gd, bf16[256,512]{1,0:T(8,128)(2,1)S(1)} %get-tuple-element.9.pgrad, ...), custom_call_target="tpu_custom_call" | custom-call | flops 1500000000 | bytes 3000000 | tf_op jit(solution)/shard_map/products/pallas_call | solution.py:502
